TPU v7x, 128 devices: a whole 4x4x4 slice. The times are simulated.
128 devices in a mesh: gz: 16 (over y_lo, x, core), head: 2 (over y_hi), tile: 4 (over z).
Axes of the slice: x: 4, y: 4 (y_hi: 2, y_lo: 2; y = y_hi * 2 + y_lo), z: 4, core: 2. Of those that a mesh axis runs over, the one named last changes fastest.
Arguments:
- nodes_in: bfloat16 [524288, 256], P(('gz', 'tile')), may hold values from -6 to 6
- cotangent: bfloat16 [524288, 256], P(('gz', 'tile')), may hold values from -6 to 6
- w_query: bfloat16 [256, 256], P(None, 'head'), may hold values from -0.375 to 0.375
- w_key: bfloat16 [256, 256], P(None, 'head'), may hold values from -0.375 to 0.375
- w_value: bfloat16 [256, 256], P(None, 'head'), may hold values from -0.375 to 0.375
- w_out: bfloat16 [256, 256], P('head'), may hold values from -0.375 to 0.375
- counts: int32 [4096], replicated, may hold values from 4 to 128
Outputs:
- output: bfloat16 [524288, 256], P(('gz', 'tile'), 'head')
- grad_nodes: bfloat16 [524288, 256], P(('gz', 'tile'), 'head')
- grad_query: float32 [256, 256], P(None, 'head')
- grad_key: float32 [256, 256], P(None, 'head')
- grad_value: float32 [256, 256], P(None, 'head')
- grad_out: float32 [256, 256], P('head')
Inputs may be any that keep to these rules, and one draw needn't show every extreme that they name: counts[b] is how many of the nodes b * 128 to (b + 1) * 128 - 1 are valid; the valid ones are the first of them.
All inputs are finite; a program needn't handle non-finite values.
Results may differ from a plain program's by a relative error of at most 0.012.
The roundings to bfloat16 on the way count: a program that leaves them out, or rounds other values in their place, can miss the bound.
Values may be sent and summed in bfloat16 or wider, within the bound.
No kernel may reach another device: no remote copies, remote signals or barrier semaphores. Data moves between devices by JAX's collectives and lax.ppermute only.
A program may use at most 128 MiB of HBM per device.

v0:
```python
import jax
import jax.numpy as jnp
from jax import lax
from jax.sharding import PartitionSpec as P

HEADS = 8
WINDOW = 128


def passed_along(block, axis, distance):
    devices = range(lax.axis_size(axis))
    route = [((i - distance) % len(devices), i) for i in devices]
    return lax.ppermute(block, axis, route)


def window_core(queries, key_block, values, valid_keys, dcontext, score_scale):
    scores = (
        jnp.einsum("whqe,whke->whqk", queries, key_block, preferred_element_type=jnp.float32)
        * score_scale
    )
    weights = jnp.exp(scores) * valid_keys[:, None, None, :]
    attention = weights / jnp.sum(weights, axis=-1, keepdims=True)
    attention_low = attention.astype(jnp.bfloat16)
    context = jnp.einsum(
        "whqk,whke->whqe", attention_low, values, preferred_element_type=jnp.float32
    ).astype(jnp.bfloat16)
    dattention = jnp.einsum("whqe,whke->whqk", dcontext, values, preferred_element_type=jnp.float32)
    center = jnp.sum(attention * dattention, axis=-1, keepdims=True)
    dscores = (attention * (dattention - center)).astype(jnp.bfloat16)
    dvalues = jnp.einsum(
        "whqk,whqe->whke", attention_low, dcontext, preferred_element_type=jnp.float32
    ).astype(jnp.bfloat16)
    dqueries = (
        score_scale
        * jnp.einsum("whqk,whke->whqe", dscores, key_block, preferred_element_type=jnp.float32)
    ).astype(jnp.bfloat16)
    key_grads = (
        score_scale
        * jnp.einsum("whqk,whqe->whke", dscores, queries, preferred_element_type=jnp.float32)
    ).astype(jnp.bfloat16)
    return (context, dqueries, key_grads, dvalues)


def to_windows(array, dilation, head_dim):
    length, columns = array.shape
    head_count = columns // head_dim
    shaped = array.reshape(length // (WINDOW * dilation), WINDOW, dilation, head_count, head_dim)
    return shaped.transpose(0, 2, 3, 1, 4).reshape(-1, head_count, WINDOW, head_dim)


def mask_windows(valid_rows, dilation):
    length = valid_rows.shape[0]
    shaped = valid_rows.reshape(length // (WINDOW * dilation), WINDOW, dilation)
    return shaped.transpose(0, 2, 1).reshape(-1, WINDOW)


def from_windows(array, dilation, length):
    head_count = array.shape[1]
    head_dim = array.shape[3]
    shaped = array.reshape(length // (WINDOW * dilation), dilation, head_count, WINDOW, head_dim)
    return shaped.transpose(0, 3, 1, 2, 4).reshape(length, head_count * head_dim)


def dilated_local(block_list, valid_rows, dilation, head_dim, score_scale):
    windowed = [to_windows(array, dilation, head_dim) for array in block_list]
    valid_win = mask_windows(valid_rows, dilation)
    results = window_core(
        windowed[0], windowed[1], windowed[2], valid_win, windowed[3], score_scale
    )
    length = valid_rows.shape[0]
    return [from_windows(result, dilation, length) for result in results]


def group_attention(projected, valid_ext, own_rows, reach, head_dim, score_scale):
    group_width = projected[0].shape[1]
    near_width = group_width // 2
    near_start = reach - WINDOW // 2
    near_length = own_rows + WINDOW
    near_parts = [array[near_start : near_start + near_length, :near_width] for array in projected]
    near_out = dilated_local(
        near_parts, valid_ext[near_start : near_start + near_length], 1, head_dim, score_scale
    )
    near_out = [array[WINDOW // 2 : WINDOW // 2 + own_rows] for array in near_out]
    far_parts = [array[:, near_width:] for array in projected]
    far_out = dilated_local(far_parts, valid_ext, 4, head_dim, score_scale)
    far_out = [array[reach : reach + own_rows] for array in far_out]
    return [
        jnp.concatenate([near_part, far_part], 1) for near_part, far_part in zip(near_out, far_out)
    ]


def project_all(ext_nodes, ext_cot, w_query, w_key, w_value, w_out):
    query_ext = jnp.dot(ext_nodes, w_query, preferred_element_type=jnp.float32).astype(jnp.bfloat16)
    key_ext = jnp.dot(ext_nodes, w_key, preferred_element_type=jnp.float32).astype(jnp.bfloat16)
    value_ext = jnp.dot(ext_nodes, w_value, preferred_element_type=jnp.float32).astype(jnp.bfloat16)
    dcontext_ext = lax.dot_general(
        ext_cot, w_out, (((1,), (1,)), ((), ())), preferred_element_type=jnp.float32
    ).astype(jnp.bfloat16)
    return (query_ext, key_ext, value_ext, dcontext_ext)


def input_terms(dqueries, key_grads, dvalues, w_query, w_key, w_value):
    contract_cols = (((1,), (1,)), ((), ()))
    grad_terms = lax.dot_general(
        dqueries, w_query, contract_cols, preferred_element_type=jnp.float32
    )
    grad_terms = grad_terms + lax.dot_general(
        key_grads, w_key, contract_cols, preferred_element_type=jnp.float32
    )
    grad_terms = grad_terms + lax.dot_general(
        dvalues, w_value, contract_cols, preferred_element_type=jnp.float32
    )
    return grad_terms


def head_group_grads(grad_terms):
    return lax.psum_scatter(
        grad_terms.astype(jnp.bfloat16), "head", scatter_dimension=1, tiled=True
    )


def weight_terms(own_nodes, own_cot, context, dqueries, key_grads, dvalues, norm):
    contract_rows = (((0,), (0,)), ((), ()))
    grad_query = (
        lax.dot_general(own_nodes, dqueries, contract_rows, preferred_element_type=jnp.float32)
        * norm
    )
    grad_key = (
        lax.dot_general(own_nodes, key_grads, contract_rows, preferred_element_type=jnp.float32)
        * norm
    )
    grad_value = (
        lax.dot_general(own_nodes, dvalues, contract_rows, preferred_element_type=jnp.float32)
        * norm
    )
    grad_out = (
        lax.dot_general(context, own_cot, contract_rows, preferred_element_type=jnp.float32) * norm
    )
    return (grad_query, grad_key, grad_value, grad_out)


def per_device(nodes_in, cotangent, w_query, w_key, w_value, w_out, counts):
    row_count = nodes_in.shape[0]
    width = nodes_in.shape[1]
    head_dim = width // HEADS
    score_scale = head_dim ** (-0.5)
    reach = 2 * WINDOW
    first_rims = jnp.concatenate([nodes_in[:reach], cotangent[:reach]], 1)
    last_rims = jnp.concatenate([nodes_in[row_count - reach :], cotangent[row_count - reach :]], 1)
    from_next = passed_along(first_rims, ("gz", "tile"), -1)
    from_prev = passed_along(last_rims, ("gz", "tile"), 1)
    ext_nodes = jnp.concatenate([from_prev[:, :width], nodes_in, from_next[:, :width]], 0)
    ext_cot_raw = jnp.concatenate([from_prev[:, width:], cotangent, from_next[:, width:]], 0)
    position = lax.axis_index(("gz", "tile"))
    block_total = counts.shape[0]
    ext_blocks = row_count // WINDOW + 4
    first_block = position * (row_count // WINDOW) - 2
    block_ids = (first_block + jnp.arange(ext_blocks, dtype=jnp.int32)) % block_total
    ext_counts = jnp.take(counts, block_ids)
    valid_ext = (
        (jnp.arange(WINDOW, dtype=jnp.int32)[None, :] < ext_counts[:, None])
        .astype(jnp.float32)
        .reshape(-1)
    )
    ext_cot = ext_cot_raw * valid_ext.astype(jnp.bfloat16)[:, None]
    norm = float(row_count * lax.axis_size(("gz", "tile"))) ** (-0.5)
    projected = project_all(ext_nodes, ext_cot, w_query, w_key, w_value, w_out)
    context, dqueries, key_grads, dvalues = group_attention(
        projected, valid_ext, row_count, reach, head_dim, score_scale
    )
    own_valid = valid_ext[reach : reach + row_count]
    own_cot = ext_cot[reach : reach + row_count]
    terms = jnp.dot(context, w_out, preferred_element_type=jnp.float32) * own_valid[:, None]
    output = lax.psum_scatter(terms, "head", scatter_dimension=1, tiled=True).astype(jnp.bfloat16)
    grad_nodes = head_group_grads(
        input_terms(dqueries, key_grads, dvalues, w_query, w_key, w_value)
    )
    grad_query, grad_key, grad_value, grad_out = weight_terms(
        nodes_in, own_cot, context, dqueries, key_grads, dvalues, norm
    )
    grad_query, grad_key, grad_value, grad_out = lax.psum(
        (grad_query, grad_key, grad_value, grad_out), ("gz", "tile")
    )
    return (output, grad_nodes, grad_query, grad_key, grad_value, grad_out)


def solution(mesh):
    return jax.shard_map(
        per_device,
        mesh=mesh,
        in_specs=(
            P(("gz", "tile"), None),
            P(("gz", "tile"), None),
            P(None, "head"),
            P(None, "head"),
            P(None, "head"),
            P("head", None),
            P(),
        ),
        out_specs=(
            P(("gz", "tile"), "head"),
            P(("gz", "tile"), "head"),
            P(None, "head"),
            P(None, "head"),
            P(None, "head"),
            P("head", None),
        ),
        check_vma=False,
    )
```

profile of v0, /device:TPU:17, one launch (start us, length us, event | category | flops | bytes accessed | tf_op | source)
XLA Modules:
  0.0 869.8 jit_solution(16001708093685585090)
XLA Ops:
  9.2 4.4 collective-permute-start.1
  27.9 5.5 convolution_convert_fusion.1
  35.1 5.2 convolution_convert_fusion.3
  43.7 9.5 %maximum_multiply_fusion = bf16[8704,256]{1,0:T(8,128)(2,1)S(1)} fusion(bf16[256,256]{1,0:T(8,128)(2,1)S(1)} %get-tuple-element.34, bf16[8192,256]{1,0:T(8,128)(2,1)S(1)} %copy-done.4, bf16[256,256]{1,0:T(8,128)(2,1)S(1)} %get-tuple-element.32, bf16[8704]{0:T(1024)(128)(2,1)S(1)} %get-tuple-element.36), kind=kLoop, calls=%fused_computation.20 | loop fusion | flops 17825792 | bytes 8930304 | tf_op jit(solution)/shard_map/mul | solution.py:165
  64.9 5.1 fusion.4
  70.0 4.5 fusion.27
  78.1 3.8 multiply_reduce_fusion.1
  81.9 4.6 multiply_convert_fusion.1
  102.5 10.1 %copy.73 = bf16[17,4,2,128,32]{3,4,2,1,0:T(8,128)(2,1)S(1)} copy(bf16[17,4,2,128,32]{4,2,1,3,0:T(2,128)(2,1)} %bitcast.151) | data formatting | bytes 2228224 | tf_op jit(solution)/shard_map/transpose | solution.py:48
  112.6 8.5 reshape.220
  121.1 10.5 %copy.77 = bf16[17,4,2,128,32]{3,4,2,1,0:T(8,128)(2,1)} copy(bf16[17,4,2,128,32]{4,2,1,3,0:T(2,128)(2,1)} %bitcast.152) | data formatting | bytes 2228224 | tf_op jit(solution)/shard_map/transpose | solution.py:48
  131.7 8.5 reshape.218
  140.2 10.2 %copy.75 = bf16[17,4,2,128,32]{3,4,2,1,0:T(8,128)(2,1)S(1)} copy(bf16[17,4,2,128,32]{4,2,1,3,0:T(2,128)(2,1)} %bitcast.153) | data formatting | bytes 2228224 | tf_op jit(solution)/shard_map/transpose | solution.py:48
  152.9 8.5 reshape.228
  161.4 10.1 %copy.85 = bf16[17,4,2,128,32]{3,4,2,1,0:T(8,128)(2,1)S(1)} copy(bf16[17,4,2,128,32]{4,2,1,3,0:T(2,128)(2,1)} %bitcast.154) | data formatting | bytes 2228224 | tf_op jit(solution)/shard_map/transpose | solution.py:48
  174.8 4.0 fusion.18
  181.9 3.8 multiply_reduce_fusion
  195.2 8.0 copy.87
  203.2 7.2 reshape.231
  217.5 4.6 fusion.38
  228.6 7.9 copy.79
  236.5 7.2 reshape.223
  247.9 7.9 copy.97
  255.8 7.2 reshape.239
  267.1 7.9 copy.92
  275.0 7.2 reshape.235
  289.6 8.1 convolution_add_fusion.1
  302.1 6.6 fusion
  308.7 6.4 copy.110
  316.6 5.9 convolution_multiply_fusion
  322.5 526.1 %all-reduce.3.cloned.1.call-done = (f32[256,128]{0,1:T(8,128)}, f32[256,128]{0,1:T(8,128)}, f32[256,128]{0,1:T(8,128)}, f32[128,256]{1,0:T(8,128)}) async-done(((f32[256,128]{0,1:T(8,128)}, f32[256,128]{0,1:T(8,128)}, f32[256,128]{0,1:T(8,128)}, f32[128,256]{1,0:T(8,128)}), (f32[256,128]{0,1:T(8,128)}, f32[256,128]{0,1:T(8,128)}, f32[256,128]{0,1:T(8,128)}, ...) | async-done | bytes 524304 | tf_op jit(solution)/shard_map/psum | solution.py:181
  853.6 4.1 copy.111
  (163 shorter events, 114.5 us)
Async XLA Ops:
  8.0 27.1 %copy-start = (bf16[256,128]{1,0:T(8,128)(2,1)S(1)}, bf16[256,128]{1,0:T(8,128)(2,1)}, u32[]{:S(2)}) copy-start(bf16[256,128]{1,0:T(8,128)(2,1)} %param.9) | copy-start | bytes 196612
  8.0 840.6 %all-reduce.3.cloned.1.call-start = ((), (), s32[]{:S(2)}) async-start(), calls=%async_computation.4 | async-start | bytes 1048576 | tf_op jit(solution)/shard_map/psum | solution.py:181
  9.2 10.5 %collective-permute-start.1 = (bf16[256,512]{1,0:T(8,128)(2,1)S(1)}, bf16[256,512]{1,0:T(8,128)(2,1)S(1)}, u32[]{:S(2)}, u32[]{:S(2)}) collective-permute-start(bf16[256,512]{1,0:T(8,128)(2,1)S(1)} %pad_maximum_fusion.28), channel_id=1, source_target_pairs={{1,0},{2,1},{3,2},{8,3},{9,8},{10,9},{11,10},{16,11},{17,16},{18,1... | collective-permute-start | bytes 786440 | tf_op jit(solution)/shard_map/ppermute | solution.py:13
  13.6 7.1 collective-permute-start
  24.5 9.0 %copy-start.6 = (bf16[8704,128]{0,1:T(8,128)(2,1)}, bf16[8704,128]{0,1:T(8,128)(2,1)S(1)}, u32[]{:S(2)}) copy-start(bf16[8704,128]{0,1:T(8,128)(2,1)S(1)} %convolution_convert_fusion.2) | copy-start | bytes 6684676
  24.5 3.4 copy-start.31
  33.5 6.8 copy-start.7
  40.3 12.9 %copy-start.8 = (bf16[8704,128]{0,1:T(8,128)(2,1)}, bf16[8704,128]{0,1:T(8,128)(2,1)S(1)}, u32[]{:S(2)}) copy-start(bf16[8704,128]{0,1:T(8,128)(2,1)S(1)} %convolution_convert_fusion.3) | copy-start | bytes 6684676
  40.3 3.4 copy-start.4
  43.7 9.6 %copy-start.24 = (bf16[128,256]{1,0:T(8,128)(2,1)S(1)}, bf16[128,256]{1,0:T(8,128)(2,1)}, u32[]{:S(2)}) copy-start(bf16[128,256]{1,0:T(8,128)(2,1)} %param.12) | copy-start | bytes 196612
  55.4 5.5 copy-start.2
  70.0 4.5 copy-start.18
  81.9 4.6 copy-start.3
  89.8 4.7 slice-start.4
  92.0 4.9 slice-start.5
  140.2 10.2 %slice-start.2 = ((bf16[8704,128]{0,1:T(8,128)(2,1)}), bf16[8704,64]{0,1:T(8,128)(2,1)S(1)}, s32[]{:S(2)}) async-start(bf16[8704,128]{0,1:T(8,128)(2,1)} %copy-done.2), calls=%async_computation.7 | async-start | bytes 2228224 | tf_op jit(solution)/shard_map/slice | solution.py:84
  174.8 4.0 copy-start.21
  217.5 4.6 copy-start.23
  222.9 3.5 copy-start.9
  225.1 3.5 copy-start.20
  243.7 4.1 copy-start.19
  263.0 4.1 copy-start.5
  282.2 3.6 copy-start.13
  285.9 3.7 copy-start.27
  285.9 11.8 %slice-start = ((s8[4456448]{0:T(1024)(128)(4,1)}), s8[4194304]{0:T(1024)(128)(4,1)S(1)}, s32[]{:S(2)}) async-start(s8[4456448]{0:T(1024)(128)(4,1)} %bitcast.149), calls=%async_computation.5 | async-start | bytes 8388608
  289.6 8.1 slice-start.1
  289.6 8.1 copy-start.14
  289.6 8.1 copy-start.16
  297.7 2.9 copy-start.32
  302.1 551.5 %reduce-scatter.7.cloned.1.call-start = ((), (), s32[]{:S(2)}) async-start(), calls=%async_computation.3 | async-start | bytes 6291456
  315.1 542.5 %reduce-scatter.5.cloned.1.call-start = ((), (), s32[]{:S(2)}) async-start(), calls=%async_computation.2 | async-start | bytes 12582912 | tf_op jit(solution)/shard_map/reduce_scatter | solution.py:174
  857.6 3.8 copy-start.26
  (12 other events, 18.7 us)
Sparse Core Ops, SparseCore 0:
  302.2 546.3 all-reduce.2
Sparse Core Ops, SparseCore 1:
  315.2 56.7 reduce-scatter.6
  374.4 102.5 reduce-scatter.4
where the time goes:
time: 878 us; the launch traced here: 870 us
  waiting for transfers between devices  530 us (60%)
  local copies, waits for them, and re-layouts  204 us (23%)
  matrix products  92.7 us (11%)
  other arithmetic  22.2 us (3%)
  between operations  16.4 us (2%)
    psum x1, waiting for transfers between devices, per_device(): lax.psum((grad_query, grad_key, grad_value, grad_out), ('gz', 'tile'))  526 us
    transpose x4, local copies, waits for them, and re-layouts, to_windows(): shaped.transpose(0, 2, 3, 1, 4).reshape(-1, head_count, WINDOW, head_dim)  40.9 us
    reshape x8, local copies, waits for them, and re-layouts, to_windows(): array.reshape(length // (WINDOW * dilation), WINDOW, dilation, head_count...  36.9 us
    unnamed x84, local copies, waits for them, and re-layouts  33.9 us
    reshape x4, local copies, waits for them, and re-layouts, from_windows(): array.reshape(length // (WINDOW * dilation), dilation, head_count, WINDOW...  31.7 us
    reshape x4, local copies, waits for them, and re-layouts, from_windows(): shaped.transpose(0, 3, 1, 2, 4).reshape(length, head_count * head_dim)  28.7 us
  transfers between devices with their start and end apart: 5, of which 3 were waited for; matrix products, arithmetic and copies ran while one was open for 4% of the time, Pallas kernels for 0%

commit v1 on v0

v1 whole, which is shorter than its diff:
```python
import math

import jax
import jax.numpy as jnp
from jax import lax
from jax.experimental import pallas as pl
from jax.experimental.pallas import tpu as pltpu
from jax.sharding import PartitionSpec as P

HEADS = 8
WINDOW = 128
HALO = 256
GROUP = 512
HEAD_DIM = 32
SCALE = HEAD_DIM ** (-0.5)
EXP2_SCALE = SCALE * math.log2(math.e)
BF = jnp.bfloat16
F32 = jnp.float32


def mm(a, b):
    return jnp.dot(a, b, preferred_element_type=F32)


def mm_nt(a, b):
    return lax.dot_general(a, b, (((1,), (1,)), ((), ())), preferred_element_type=F32)


def head_spread(block):
    lane_head = lax.broadcasted_iota(jnp.int32, block.shape, 1) // HEAD_DIM
    zero = jnp.zeros_like(block)
    return jnp.concatenate([jnp.where(lane_head == h, block, zero) for h in range(4)], 0)


def windows_core(loaded, masks):
    spread_q = [head_spread(q) for q, k, v, d in loaded]
    spread_d = [head_spread(d) for q, k, v, d in loaded]
    scores = [mm_nt(w[1], sq) for w, sq in zip(loaded, spread_q)]
    datt = [mm_nt(w[2], sd) for w, sd in zip(loaded, spread_d)]
    low, dsc = [], []
    for s, da, mask in zip(scores, datt, masks):
        low_parts, dsc_parts = [], []
        for h in range(4):
            cols = slice(h * WINDOW, (h + 1) * WINDOW)
            e = jnp.where(mask, jnp.exp2(s[:, cols] * EXP2_SCALE), 0.0)
            a = e * (1.0 / jnp.sum(e, axis=0, keepdims=True))
            d = da[:, cols]
            center = jnp.sum(a * d, axis=0, keepdims=True)
            low_parts.append(a.astype(BF))
            dsc_parts.append((a * (d - center)).astype(BF))
        low.append(low_parts)
        dsc.append(dsc_parts)
    results = []
    for (q, k, v, d), sq, sd, lw, ds in zip(loaded, spread_q, spread_d, low, dsc):
        lw_all = jnp.concatenate(lw, 1)
        ds_all = jnp.concatenate(ds, 1)
        dv = mm(lw_all, sd)
        dk = mm(ds_all, sq) * SCALE
        k_t, v_t = k.T, v.T
        ctx_t, dq_t = [], []
        for pair in range(2):
            rows = slice(pair * 64, pair * 64 + 64)
            cols = slice(pair * 256, pair * 256 + 256)
            c2 = mm(v_t[rows], lw_all[:, cols])
            q2 = mm(k_t[rows], ds_all[:, cols])
            ctx_t += [c2[:32, :128], c2[32:, 128:]]
            dq_t += [q2[:32, :128], q2[32:, 128:]]
        ctx = jnp.concatenate(ctx_t, 0).T
        dq = jnp.concatenate(dq_t, 0).T * SCALE
        results.append((ctx, dq, dk, dv))
    return results


def local_kernel(rows, use_halo, norm, *refs):
    meta, counts = refs[:2]
    refs = refs[2:]
    if use_halo:
        x_hbm, c_hbm, halo_hbm, own_ref, oth_ref, g_in = refs[:6]
        refs = refs[6:]
    else:
        x_hbm, c_hbm, own_ref, oth_ref = refs[:4]
        refs = refs[4:]
    (out_keep, out_send, gn_keep, gn_send, g_out) = refs[:5]
    (xs, cs, near_in, near_out, far_out, far_stage, far_res, wqkv, wqkv_t, wout_t, wout_p, gacc, gacc_o, sems) = refs[5:]
    ext = rows + 2 * HALO
    first_block = meta[0]
    side = meta[1]
    src = pl.multiple_of(meta[2], HALO)
    block_mask = counts.shape[0]

    def count_of(block):
        return counts[lax.rem(first_block + block, block_mask)]

    copies = []
    if use_halo:
        main = ext - HALO
        dst = pl.multiple_of((1 - side) * HALO, HALO)
        hdst = pl.multiple_of(side * main, HALO)
        width = xs.shape[1]
        copies.append(pltpu.make_async_copy(x_hbm.at[pl.ds(src, main)], xs.at[pl.ds(dst, main)], sems.at[0]))
        copies.append(pltpu.make_async_copy(c_hbm.at[pl.ds(src, main)], cs.at[pl.ds(dst, main)], sems.at[1]))
        copies.append(pltpu.make_async_copy(halo_hbm.at[:, pl.ds(0, width)], xs.at[pl.ds(hdst, HALO)], sems.at[2]))
        copies.append(pltpu.make_async_copy(halo_hbm.at[:, pl.ds(width, width)], cs.at[pl.ds(hdst, HALO)], sems.at[3]))
    else:
        copies.append(pltpu.make_async_copy(x_hbm.at[pl.ds(src, ext)], xs, sems.at[0]))
        copies.append(pltpu.make_async_copy(c_hbm.at[pl.ds(src, ext)], cs, sems.at[1]))
    for copy in copies:
        copy.start()

    for part in range(2):
        cols = slice(part * 64, part * 64 + 64)
        for j in range(3):
            in_rows = slice(j * 256, j * 256 + 256)
            wqkv[:, part * 384 + j * 128 : part * 384 + j * 128 + 128] = jnp.concatenate(
                [own_ref[in_rows, cols], oth_ref[in_rows, cols]], 1
            )
        for pos, half in enumerate((own_ref, oth_ref)):
            dst_rows = slice(part * 128 + pos * 64, part * 128 + pos * 64 + 64)
            for col in range(2):
                natural = half[768 + 128 * col + part * 64 : 768 + 128 * col + part * 64 + 64, :]
                wout_t[dst_rows, col * 128 : col * 128 + 128] = natural
                turn = jnp.where(side == 0, col, 1 - col)
                start = pl.multiple_of(768 + 128 * turn + part * 64, 64)
                wout_p[dst_rows, col * 128 : col * 128 + 128] = half[pl.ds(start, 64), :]
    wout_t[...] = wout_t[...].T
    wq_own = wqkv[pl.ds(pl.multiple_of(side * 128, 128), 128), :]
    wq_oth = wqkv[pl.ds(pl.multiple_of((1 - side) * 128, 128), 128), :]
    wqkv_t[:, 0:128] = wq_own.T
    wqkv_t[:, 128:256] = wq_oth.T
    gacc[...] = jnp.zeros_like(gacc)
    gacc_o[...] = jnp.zeros_like(gacc_o)
    for copy in copies:
        copy.wait()

    row_iota = lax.broadcasted_iota(jnp.int32, (WINDOW, WINDOW), 0)

    def far_group(g, _):
        base = pl.multiple_of(g * GROUP, GROUP)
        x = xs[pl.ds(base, GROUP), :]
        for b in range(4):
            valid = lax.broadcasted_iota(jnp.int32, (WINDOW, 256), 0) < count_of(4 * g + b)
            piece = pl.ds(pl.multiple_of(base + b * WINDOW, WINDOW), WINDOW)
            cs[piece, :] = jnp.where(valid, cs[piece, :].astype(F32), 0.0).astype(BF)
        c = cs[pl.ds(base, GROUP), :]
        proj = mm(x, wqkv[...])
        dctx = mm(c, wout_t[...])
        near_in[pl.ds(base, GROUP), 0:384] = proj[:, 0:384].astype(BF)
        near_in[pl.ds(base, GROUP), 384:512] = dctx[:, 0:128].astype(BF)
        for j in range(3):
            far_stage[j] = proj[:, 384 + 128 * j : 512 + 128 * j]
        far_stage[3] = dctx[:, 128:256]
        loaded, masks = [], []
        for r in range(4):
            loaded.append([far_stage[j, pl.ds(r, WINDOW, stride=4), :].astype(BF) for j in range(4)])
            quarter = row_iota // 32
            limit = jnp.where(
                quarter < 2,
                jnp.where(quarter == 0, count_of(4 * g), count_of(4 * g + 1)),
                jnp.where(quarter == 2, count_of(4 * g + 2), count_of(4 * g + 3)),
            )
            masks.append(4 * (row_iota - 32 * quarter) + r < limit)
        for r, result in enumerate(windows_core(loaded, masks)):
            for j in range(4):
                far_res[j, pl.ds(r, WINDOW, stride=4), :] = result[j]
        for j in range(4):
            far_out[pl.ds(base, GROUP), 128 * j : 128 * j + 128] = far_res[j].astype(BF)
        return 0

    lax.fori_loop(0, ext // GROUP, far_group, 0)

    def near_windows(first, count):
        loaded, masks, places = [], [], []
        for i in range(count):
            w = first + i
            place = pl.ds(pl.multiple_of(192 + 128 * w, 64), WINDOW)
            block = near_in[place, :]
            loaded.append([block[:, 128 * j : 128 * j + 128] for j in range(4)])
            limit = jnp.where(row_iota < 64, count_of(w + 1) - 64, count_of(w + 2) + 64)
            masks.append(row_iota < limit)
            places.append(place)
        for place, result in zip(places, windows_core(loaded, masks)):
            for j in range(4):
                near_out[place, 128 * j : 128 * j + 128] = result[j].astype(BF)

    def near_step(s, _):
        near_windows(4 * s, 4)
        return 0

    total_near = rows // WINDOW + 1
    lax.fori_loop(0, total_near // 4, near_step, 0)
    if total_near % 4:
        near_windows(total_near // 4 * 4, total_near % 4)

    def finish(b, _):
        here = pl.ds(pl.multiple_of(HALO + GROUP * b, HALO), GROUP)
        there = pl.ds(pl.multiple_of(GROUP * b, GROUP), GROUP)
        near = near_out[here, :]
        far = far_out[here, :]
        ctx = jnp.concatenate([near[:, :128], far[:, :128]], 1)
        grads = jnp.concatenate([near[:, 128:], far[:, 128:]], 1)
        out = mm(ctx, wout_p[...])
        parts = []
        for q in range(4):
            valid = lax.broadcasted_iota(jnp.int32, (WINDOW, 256), 0) < count_of(4 * b + 2 + q)
            parts.append(jnp.where(valid, out[q * WINDOW : (q + 1) * WINDOW], 0.0))
        out = jnp.concatenate(parts, 0).astype(BF)
        out_keep[there, :] = out[:, :128]
        out_send[there, :] = out[:, 128:]
        gn = mm(grads, wqkv_t[...]).astype(BF)
        gn_keep[there, :] = gn[:, :128]
        gn_send[there, :] = gn[:, 128:]
        gacc[...] += mm(xs[here, :].T, grads)
        gacc_o[...] += mm(ctx.T, cs[here, :])
        return 0

    lax.fori_loop(0, rows // GROUP, finish, 0)

    for pos in range(2):
        half = side if pos == 0 else 1 - side
        for j in range(3):
            near = gacc[:, 128 * j + 64 * pos : 128 * j + 64 * pos + 64]
            far = gacc[:, 384 + 128 * j + 64 * pos : 384 + 128 * j + 64 * pos + 64]
            g_out[half, 256 * j : 256 * j + 256, :] = jnp.concatenate([near, far], 1) * norm
        for part in range(2):
            for col in range(2):
                piece = gacc_o[128 * part + 64 * pos : 128 * part + 64 * pos + 64, 128 * col : 128 * col + 128]
                low = 768 + 128 * col + 64 * part
                g_out[half, low : low + 64, :] = piece * norm
    if use_halo:
        g_out[...] = g_out[...] + g_in[...]


def local_call(rows, norm, meta, counts, nodes_in, cotangent, own, oth, halo=None, g_in=None):
    ext = rows + 2 * HALO
    use_halo = halo is not None
    vmem = pl.BlockSpec(memory_space=pltpu.VMEM)
    hbm = pl.BlockSpec(memory_space=pl.ANY)
    smem = pl.BlockSpec(memory_space=pltpu.SMEM)
    half = jax.ShapeDtypeStruct((rows, 128), BF)
    if use_halo:
        args = (meta, counts, nodes_in, cotangent, halo, own, oth, g_in)
        in_specs = [smem, smem, hbm, hbm, hbm, vmem, vmem, vmem]
    else:
        args = (meta, counts, nodes_in, cotangent, own, oth)
        in_specs = [smem, smem, hbm, hbm, vmem, vmem]

    def body(*refs):
        local_kernel(rows, use_halo, norm, *refs)

    return pl.pallas_call(
        body,
        out_shape=(half, half, half, half, jax.ShapeDtypeStruct((2, 1024, 128), F32)),
        in_specs=in_specs,
        out_specs=(vmem,) * 5,
        scratch_shapes=[
            pltpu.VMEM((ext, 256), BF),
            pltpu.VMEM((ext, 256), BF),
            pltpu.VMEM((ext, 512), BF),
            pltpu.VMEM((ext, 512), BF),
            pltpu.VMEM((ext, 512), BF),
            pltpu.VMEM((4, GROUP, 128), F32),
            pltpu.VMEM((4, GROUP, 128), F32),
            pltpu.VMEM((256, 768), BF),
            pltpu.VMEM((768, 256), BF),
            pltpu.VMEM((256, 256), BF),
            pltpu.VMEM((256, 256), BF),
            pltpu.VMEM((256, 768), F32),
            pltpu.VMEM((256, 256), F32),
            pltpu.SemaphoreType.DMA((4,)),
        ],
        compiler_params=pltpu.CompilerParams(vmem_limit_bytes=56 * 1024 * 1024),
        cost_estimate=pl.CostEstimate(flops=rows * 4000000, bytes_accessed=rows * 3000, transcendentals=0),
    )(*args)


def per_device(nodes_in, cotangent, w_query, w_key, w_value, w_out, counts):
    row_count = nodes_in.shape[0]
    quarter = row_count // 4
    side = lax.axis_index("head").astype(jnp.int32)
    place = lax.axis_index(("gz", "tile")).astype(jnp.int32)
    gz, heads, tiles = lax.axis_size("gz"), lax.axis_size("head"), lax.axis_size("tile")
    places = gz * tiles
    swap = [(0, 1), (1, 0)]

    own = jnp.concatenate([w_query, w_key, w_value, w_out[:, :128], w_out[:, 128:]], 0)
    oth = lax.ppermute(own, "head", swap)

    def flat(p, h):
        return (p // tiles * heads + h) * tiles + p % tiles

    rim = (1 - side) * (row_count - HALO)
    rims = jnp.concatenate(
        [lax.dynamic_slice_in_dim(nodes_in, rim, HALO), lax.dynamic_slice_in_dim(cotangent, rim, HALO)], 1
    )
    route = [(flat(p, 0), flat((p + 1) % places, 0)) for p in range(places)]
    route += [(flat(p, 1), flat((p - 1) % places, 1)) for p in range(places)]
    halo = lax.ppermute(rims, ("gz", "head", "tile"), route)

    norm = float(row_count * places) ** (-0.5)
    blocks = row_count // WINDOW

    def meta_of(first_row, source):
        first_block = (place * blocks + counts.shape[0] + (first_row - HALO) // WINDOW) % counts.shape[0]
        return jnp.stack([first_block, side, source]).astype(jnp.int32)

    row_a = quarter * (1 + side)
    row_b = 3 * quarter * side
    a = local_call(quarter, norm, meta_of(row_a, row_a - HALO), counts, nodes_in, cotangent, own, oth)
    sent_a = [lax.ppermute(a[1], "head", swap), lax.ppermute(a[3], "head", swap)]
    source_b = side * (row_b - HALO)
    b = local_call(
        quarter, norm, meta_of(row_b, source_b), counts, nodes_in, cotangent, own, oth, halo, a[4]
    )
    sent_b = [lax.ppermute(b[1], "head", swap), lax.ppermute(b[3], "head", swap)]

    grads = b[4].reshape(heads * places, 1024 // places, 128)
    grads = lax.all_to_all(grads, ("head", "gz", "tile"), 0, 0, tiled=True)
    share = jnp.sum(grads, axis=0)
    share = jnp.broadcast_to(share[None], (places,) + share.shape)
    whole = lax.all_to_all(share, ("gz", "tile"), 0, 0, tiled=True).reshape(1024, 128)

    other_a = quarter * (2 - side)
    other_b = 3 * quarter * (1 - side)

    def assemble(keep_a, keep_b, got_a, got_b):
        full = jnp.zeros((row_count, 128), BF)
        for rows, first in ((keep_a, row_a), (keep_b, row_b), (got_a, other_a), (got_b, other_b)):
            full = lax.dynamic_update_slice(full, rows, (first, 0))
        return full

    output = assemble(a[0], b[0], sent_a[0], sent_b[0])
    grad_nodes = assemble(a[2], b[2], sent_a[1], sent_b[1])
    grad_out = jnp.concatenate([whole[768:896], whole[896:1024]], 1)
    return (output, grad_nodes, whole[0:256], whole[256:512], whole[512:768], grad_out)


def solution(mesh):
    return jax.shard_map(
        per_device,
        mesh=mesh,
        in_specs=(
            P(("gz", "tile"), None),
            P(("gz", "tile"), None),
            P(None, "head"),
            P(None, "head"),
            P(None, "head"),
            P("head", None),
            P(),
        ),
        out_specs=(
            P(("gz", "tile"), "head"),
            P(("gz", "tile"), "head"),
            P(None, "head"),
            P(None, "head"),
            P(None, "head"),
            P("head", None),
        ),
        check_vma=False,
    )
```

time: 878 us -> 128 us (0.15)
  waiting for transfers between devices: 530 us -> 21.1 us
  local copies, waits for them, and re-layouts: 204 us -> 18 us
  matrix products: 92.7 us -> 0 us
  Pallas kernels: 0 us -> 40.7 us
  starting transfers between devices: 4.61 us -> 44.7 us
  other arithmetic: 22.2 us -> 1.99 us
  between operations: 16.4 us -> 0.76 us
    psum x1 -> x0, waiting for transfers between devices: 526 us -> none  [per_device(): lax.psum((grad_query, grad_key, grad_value, grad_out), ('gz', 'tile'))]
    reshape x16 -> x0, local copies, waits for them, and re-layouts: 97.3 us -> none  [the longest x8 36.9 us: to_windows(): array.reshape(length // (WINDOW * dilation), WINDOW, dilation, head_count...]
    dot_general x24 -> x0, matrix products: 92.7 us -> none  [the longest x2 8.5 us: window_core(): jnp.einsum('whqk,whqe->whke', attention_low, dcontext, preferred_element_...]
    transpose x8 -> x0, local copies, waits for them, and re-layouts: 43.7 us -> none  [the longest x4 40.9 us: to_windows(): shaped.transpose(0, 2, 3, 1, 4).reshape(-1, head_count, WINDOW, head_dim)]
    pallas_call x0 -> x2, Pallas kernels: none -> 40.7 us  [local_call(): pl.pallas_call(body, out_shape=(half, half, half, half, jax.ShapeDtypeStr...]
    all_to_all x0 -> x2, starting transfers between devices: none -> 33.9 us  [the longest x1 21.4 us: per_device(): lax.all_to_all(share, ('gz', 'tile'), 0, 0, tiled=True).reshape(1024, 128)]
    unnamed x84 -> x20, local copies, waits for them, and re-layouts: 33.9 us -> 4.97 us
    slice x27 -> x2, local copies, waits for them, and re-layouts: 26.7 us -> 0.76 us  [the longest x1 0.75 us: per_device(): whole[512:768]]
  transfers between devices with their start and end apart: 5 -> 8, of which waited for: 3 -> 3; matrix products, arithmetic and copies ran while one was open for 4% -> 10% of each run, Pallas kernels for 0% -> 32%
where the time goes in v1:
time: 128 us; the launch traced here: 127 us
  starting transfers between devices  44.7 us (35%)
  Pallas kernels  40.7 us (32%)
  waiting for transfers between devices  21.1 us (16%)
  local copies, waits for them, and re-layouts  18 us (14%)
  other arithmetic  1.99 us (2%)
    pallas_call x2, Pallas kernels, local_call(): pl.pallas_call(body, out_shape=(half, half, half, half, jax.ShapeDtypeStr...  40.7 us
    all_to_all x1, starting transfers between devices, per_device(): lax.all_to_all(share, ('gz', 'tile'), 0, 0, tiled=True).reshape(1024, 128)  21.4 us
    all_to_all x1, starting transfers between devices, per_device(): grads = lax.all_to_all(grads, ('head', 'gz', 'tile'), 0, 0, tiled=True)  12.4 us
    all_to_all x1, waiting for transfers between devices, per_device(): grads = lax.all_to_all(grads, ('head', 'gz', 'tile'), 0, 0, tiled=True)  10.9 us
    all_to_all x1, waiting for transfers between devices, per_device(): lax.all_to_all(share, ('gz', 'tile'), 0, 0, tiled=True).reshape(1024, 128)  8.42 us
    dynamic_update_slice x8, local copies, waits for them, and re-layouts, assemble(): full = lax.dynamic_update_slice(full, rows, (first, 0))  7.77 us
    unnamed x20, local copies, waits for them, and re-layouts  4.97 us
    ppermute x1, starting transfers between devices, per_device(): halo = lax.ppermute(rims, ('gz', 'head', 'tile'), route)  4.62 us
  transfers between devices with their start and end apart: 8, of which 3 were waited for; matrix products, arithmetic and copies ran while one was open for 10% of the time, Pallas kernels for 32%

profile of v1, /device:TPU:17, one launch (start us, length us, event | category | flops | bytes accessed | tf_op | source)
XLA Modules:
  0.0 127.3 jit_solution(14651373700087075176)
XLA Ops:
  0.6 0.8 constant_dynamic-update-slice_fusion.2
  1.5 0.9 constant_dynamic-update-slice_fusion.1
  2.3 0.9 constant_dynamic-update-slice_fusion
  3.2 0.8 slice_dynamic-update-slice_fusion.1
  4.0 0.8 slice_dynamic-update-slice_fusion.refs_4_.refs_5_
  4.7 1.1 constant_dynamic-slice_fusion
  5.8 4.6 %collective-permute-start.1 = (bf16[256,512]{1,0:T(8,128)(2,1)S(1)}, bf16[256,512]{1,0:T(8,128)(2,1)S(1)}, u32[]{:S(2)}, u32[]{:S(2)}) collective-permute-start(bf16[256,512]{1,0:T(8,128)(2,1)S(1)} %pad_maximum_fusion), channel_id=1, source_target_pairs={{0,1},{1,2},{2,3},{3,8},{8,9},{9,10},{10,11},{11,16},{16,17},{17,1... | collective-permute-start | bytes 786440 | tf_op jit(solution)/shard_map/ppermute | solution.py:297
  10.5 0.6 pad_add_fusion.refs_0_
  11.1 0.6 pad_add_fusion.1.refs_0_
  11.6 1.8 %collective-permute-done.refs_5_.refs_6_ = bf16[1024,128]{1,0:T(8,128)(2,1)S(1)} collective-permute-done((bf16[1024,128]{1,0:T(8,128)(2,1)S(1)}, bf16[1024,128]{1,0:T(8,128)(2,1)S(1)}, u32[]{:S(2)}, u32[]{:S(2)}) %collective-permute-start) | collective-permute-done | bytes 262176 | tf_op jit(solution)/shard_map/ppermute | solution.py:286
  13.4 0.7 copy-done.6
  14.1 20.2 %shard_map.118 = (bf16[2048,128]{1,0:T(8,128)(2,1)}, bf16[2048,128]{1,0:T(8,128)(2,1)}, bf16[2048,128]{1,0:T(8,128)(2,1)}, bf16[2048,128]{1,0:T(8,128)(2,1)}, f32[2,1024,128]{2,1,0:T(8,128)}) custom-call(s32[3]{0:T(128)} %pad_add_fusion.refs_0_, s32[4096]{0:T(1024)} %refs_1_.3, bf16[8192,256]{1,0:T(8,128)(2,1)} %refs_2_.3, bf16[8192,256]{1,0:T(8,128)(2,1)} %refs_3_.3, ...), custom_call_target="tpu_custom_call" | custom-call | flops 8192000000 | bytes 6144000 | tf_op jit(solution)/shard_map/pallas_call | solution.py:250
  34.4 0.7 copy-done.7
  35.2 20.5 %shard_map.119 = (bf16[2048,128]{1,0:T(8,128)(2,1)}, bf16[2048,128]{1,0:T(8,128)(2,1)}, bf16[2048,128]{1,0:T(8,128)(2,1)}, bf16[2048,128]{1,0:T(8,128)(2,1)}, f32[2,1024,128]{2,1,0:T(8,128)}) custom-call(s32[3]{0:T(128)} %pad_add_fusion.1.refs_0_, s32[4096]{0:T(1024)} %refs_1_.3, bf16[8192,256]{1,0:T(8,128)(2,1)} %refs_2_.3, bf16[8192,256]{1,0:T(8,128)(2,1)} %refs_3_.3, ...), custom_call_target="tpu_custom_call" | custom-call | flops 8192000000 | bytes 6144000 | tf_op jit(solution)/shard_map/pallas_call | solution.py:250
  55.7 3.0 %collective-permute-start.5 = (bf16[2048,128]{1,0:T(8,128)(2,1)}, bf16[2048,128]{1,0:T(8,128)(2,1)}, u32[]{:S(2)}, u32[]{:S(2)}) collective-permute-start(bf16[2048,128]{1,0:T(8,128)(2,1)} %get-tuple-element.24), channel_id=1, source_target_pairs={{0,4},{4,0},{1,5},{5,1},{2,6},{6,2},{3,7},{7,3},{8,12},{12,8},{9,1... | collective-permute-start | bytes 1572872 | tf_op jit(solution)/shard_map/ppermute | solution.py:314
  58.7 12.4 %all-to-all-start = ((f32[128,16,128]{2,1,0:T(8,128)}), f32[128,16,128]{2,1,0:T(8,128)S(1)}, u32[]{:S(2)}, u32[]{:S(2)}) async-start(f32[128,16,128]{2,1,0:T(8,128)} %bitcast.11), calls=%async_computation | async-start | bytes 2097152 | tf_op jit(solution)/shard_map/all_to_all | solution.py:317
  71.1 0.2 collective-permute-start.2
  71.3 2.9 %collective-permute-start.3 = (bf16[2048,128]{1,0:T(8,128)(2,1)}, bf16[2048,128]{1,0:T(8,128)(2,1)}, u32[]{:S(2)}, u32[]{:S(2)}) collective-permute-start(bf16[2048,128]{1,0:T(8,128)(2,1)} %get-tuple-element.20), channel_id=1, source_target_pairs={{0,4},{4,0},{1,5},{5,1},{2,6},{6,2},{3,7},{7,3},{8,12},{12,8},{9,1... | collective-permute-start | bytes 1572872 | tf_op jit(solution)/shard_map/ppermute | solution.py:314
  74.2 1.6 %broadcast.8.clone.1 = bf16[8192,128]{1,0:T(8,128)(2,1)} broadcast(bf16[]{:T(256)} %constant.56.clone.1), dimensions={} | broadcast | bytes 2097154 | tf_op jit(solution)/shard_map/broadcast.1
  75.8 0.8 constant_dynamic-update-slice_fusion.6
  76.6 0.3 broadcast.8.clone
  77.2 0.8 constant_dynamic-update-slice_fusion.5
  78.1 1.9 %constant_dynamic-update-slice_fusion.4 = bf16[8192,128]{1,0:T(8,128)(2,1)} fusion(bf16[8192,128]{1,0:T(8,128)(2,1)} %constant_dynamic-update-slice_fusion.5, bf16[2048,128]{1,0:T(8,128)(2,1)} %collective-permute-done.4, s32[]{:T(128)S(6)} %select_n.45), kind=kLoop, calls=%fused_computation.8 | loop fusion | bytes 1048580 | tf_op jit(solution)/shard_map/dynamic_update_slice | solution.py:328
  80.0 10.9 %all-to-all-done = f32[128,16,128]{2,1,0:T(8,128)S(1)} async-done(((f32[128,16,128]{2,1,0:T(8,128)}), f32[128,16,128]{2,1,0:T(8,128)S(1)}, u32[]{:S(2)}, u32[]{:S(2)}) %all-to-all-start) | async-done | bytes 1048608 | tf_op jit(solution)/shard_map/all_to_all | solution.py:317
  91.1 0.8 broadcast_in_dim.2
  91.9 21.4 %all-to-all-start.1 = ((f32[64,16,128]{2,1,0:T(8,128)}), f32[64,16,128]{2,1,0:T(8,128)S(1)}, u32[]{:S(2)}, u32[]{:S(2)}) async-start(f32[64,16,128]{2,1,0:T(8,128)} %broadcast_in_dim.2), calls=%async_computation.1 | async-start | bytes 1048576 | tf_op jit(solution)/shard_map/all_to_all | solution.py:320
  113.3 1.1 constant_dynamic-update-slice_fusion.8
  114.5 1.9 %constant_dynamic-update-slice_fusion.3 = bf16[8192,128]{1,0:T(8,128)(2,1)} fusion(bf16[8192,128]{1,0:T(8,128)(2,1)} %constant_dynamic-update-slice_fusion.4, bf16[2048,128]{1,0:T(8,128)(2,1)} %collective-permute-done.5, s32[]{:T(128)S(6)} %select_n.46), kind=kLoop, calls=%fused_computation.7 | loop fusion | bytes 1048580 | tf_op jit(solution)/shard_map/dynamic_update_slice | solution.py:328
  116.4 1.1 constant_dynamic-update-slice_fusion.7
  117.5 8.4 %all-to-all-done.1 = f32[64,16,128]{2,1,0:T(8,128)S(1)} async-done(((f32[64,16,128]{2,1,0:T(8,128)}), f32[64,16,128]{2,1,0:T(8,128)S(1)}, u32[]{:S(2)}, u32[]{:S(2)}) %all-to-all-start.1) | async-done | bytes 524320 | tf_op jit(solution)/shard_map/all_to_all | solution.py:320
  125.9 0.7 pad_maximum_fusion.1
  126.6 0.8 fusion.1
  (26 shorter events, 0.7 us)
Async XLA Ops:
  4.7 8.7 %copy-start.5 = (bf16[1024,128]{1,0:T(8,128)(2,1)}, bf16[1024,128]{1,0:T(8,128)(2,1)S(1)}, u32[]{:S(2)}) copy-start(bf16[1024,128]{1,0:T(8,128)(2,1)S(1)} %slice_dynamic-update-slice_fusion.refs_4_.refs_5_) | copy-start | bytes 786436
  4.7 8.7 %collective-permute-start = (bf16[1024,128]{1,0:T(8,128)(2,1)S(1)}, bf16[1024,128]{1,0:T(8,128)(2,1)S(1)}, u32[]{:S(2)}, u32[]{:S(2)}) collective-permute-start(bf16[1024,128]{1,0:T(8,128)(2,1)S(1)} %slice_dynamic-update-slice_fusion.refs_4_.refs_5_), channel_id=1, source_target_pairs={{0,4},{4,0},{1,5},{5,1},{2,6},{6,2},{3,7},{7,3},{8,12},{12,8},{9,1... | collective-permute-start | bytes 786440 | tf_op jit(solution)/shard_map/ppermute | solution.py:286
  5.8 28.6 %collective-permute-start.1 = (bf16[256,512]{1,0:T(8,128)(2,1)S(1)}, bf16[256,512]{1,0:T(8,128)(2,1)S(1)}, u32[]{:S(2)}, u32[]{:S(2)}) collective-permute-start(bf16[256,512]{1,0:T(8,128)(2,1)S(1)} %pad_maximum_fusion), channel_id=1, source_target_pairs={{0,1},{1,2},{2,3},{3,8},{8,9},{9,10},{10,11},{11,16},{16,17},{17,1... | collective-permute-start | bytes 786440 | tf_op jit(solution)/shard_map/ppermute | solution.py:297
  13.4 0.7 copy-start.6
  34.3 43.8 %collective-permute-start.4 = (bf16[2048,128]{1,0:T(8,128)(2,1)}, bf16[2048,128]{1,0:T(8,128)(2,1)}, u32[]{:S(2)}, u32[]{:S(2)}) collective-permute-start(bf16[2048,128]{1,0:T(8,128)(2,1)} %get-tuple-element.23), channel_id=1, source_target_pairs={{0,4},{4,0},{1,5},{5,1},{2,6},{6,2},{3,7},{7,3},{8,12},{12,8},{9,1... | collective-permute-start | bytes 1572872 | tf_op jit(solution)/shard_map/ppermute | solution.py:309
  34.4 0.7 copy-start.7
  55.7 58.8 %collective-permute-start.5 = (bf16[2048,128]{1,0:T(8,128)(2,1)}, bf16[2048,128]{1,0:T(8,128)(2,1)}, u32[]{:S(2)}, u32[]{:S(2)}) collective-permute-start(bf16[2048,128]{1,0:T(8,128)(2,1)} %get-tuple-element.24), channel_id=1, source_target_pairs={{0,4},{4,0},{1,5},{5,1},{2,6},{6,2},{3,7},{7,3},{8,12},{12,8},{9,1... | collective-permute-start | bytes 1572872 | tf_op jit(solution)/shard_map/ppermute | solution.py:314
  58.7 17.1 %copy-start.2 = (bf16[2048,128]{1,0:T(8,128)(2,1)S(1)}, bf16[2048,128]{1,0:T(8,128)(2,1)}, u32[]{:S(2)}) copy-start(bf16[2048,128]{1,0:T(8,128)(2,1)} %get-tuple-element.21) | copy-start | bytes 1572868
  58.7 32.2 %all-to-all-start = ((f32[128,16,128]{2,1,0:T(8,128)}), f32[128,16,128]{2,1,0:T(8,128)S(1)}, u32[]{:S(2)}, u32[]{:S(2)}) async-start(f32[128,16,128]{2,1,0:T(8,128)} %bitcast.11), calls=%async_computation | async-start | bytes 2097152 | tf_op jit(solution)/shard_map/all_to_all | solution.py:317
  71.1 42.2 %collective-permute-start.2 = (bf16[2048,128]{1,0:T(8,128)(2,1)}, bf16[2048,128]{1,0:T(8,128)(2,1)}, u32[]{:S(2)}, u32[]{:S(2)}) collective-permute-start(bf16[2048,128]{1,0:T(8,128)(2,1)} %get-tuple-element.19), channel_id=1, source_target_pairs={{0,4},{4,0},{1,5},{5,1},{2,6},{6,2},{3,7},{7,3},{8,12},{12,8},{9,1... | collective-permute-start | bytes 1572872 | tf_op jit(solution)/shard_map/ppermute | solution.py:309
  71.3 45.1 %collective-permute-start.3 = (bf16[2048,128]{1,0:T(8,128)(2,1)}, bf16[2048,128]{1,0:T(8,128)(2,1)}, u32[]{:S(2)}, u32[]{:S(2)}) collective-permute-start(bf16[2048,128]{1,0:T(8,128)(2,1)} %get-tuple-element.20), channel_id=1, source_target_pairs={{0,4},{4,0},{1,5},{5,1},{2,6},{6,2},{3,7},{7,3},{8,12},{12,8},{9,1... | collective-permute-start | bytes 1572872 | tf_op jit(solution)/shard_map/ppermute | solution.py:314
  75.8 1.2 copy-start.1
  75.8 1.4 %copy-start.4 = (bf16[2048,128]{1,0:T(8,128)(2,1)S(1)}, bf16[2048,128]{1,0:T(8,128)(2,1)}, u32[]{:S(2)}) copy-start(bf16[2048,128]{1,0:T(8,128)(2,1)} %get-tuple-element.22) | copy-start | bytes 1572868
  76.6 1.4 %copy-start.3 = (bf16[2048,128]{1,0:T(8,128)(2,1)S(1)}, bf16[2048,128]{1,0:T(8,128)(2,1)}, u32[]{:S(2)}) copy-start(bf16[2048,128]{1,0:T(8,128)(2,1)} %get-tuple-element.18) | copy-start | bytes 1572868
  91.9 34.0 %all-to-all-start.1 = ((f32[64,16,128]{2,1,0:T(8,128)}), f32[64,16,128]{2,1,0:T(8,128)S(1)}, u32[]{:S(2)}, u32[]{:S(2)}) async-start(f32[64,16,128]{2,1,0:T(8,128)} %broadcast_in_dim.2), calls=%async_computation.1 | async-start | bytes 1048576 | tf_op jit(solution)/shard_map/all_to_all | solution.py:320
  117.5 9.9 %copy-start = (bf16[8192,128]{1,0:T(8,128)(2,1)}, bf16[8192,128]{1,0:T(8,128)(2,1)S(1)}, u32[]{:S(2)}) copy-start(bf16[8192,128]{1,0:T(8,128)(2,1)S(1)} %constant_dynamic-update-slice_fusion.7) | copy-start | bytes 6291460

commit v2 on v0

v2 whole, which is shorter than its diff:
```python
import functools
import math

import jax
import jax.numpy as jnp
from jax import lax
from jax.experimental import pallas as pl
from jax.experimental.pallas import tpu as pltpu
from jax.sharding import PartitionSpec as P

WINDOW = 128
HALO = 256
GROUP = 512
HEAD_DIM = 32
CALL_GROUPS = (3, 3, 3)
BEYOND = 3
SCALE = HEAD_DIM ** (-0.5)
EXP2_SCALE = SCALE * math.log2(math.e)
VMEM_LIMIT = 56 * 1024 * 1024
BF = jnp.bfloat16
F32 = jnp.float32


def mm(a, b):
    return jnp.dot(a, b, preferred_element_type=F32)


def mm_nt(a, b):
    return lax.dot_general(a, b, (((1,), (1,)), ((), ())), preferred_element_type=F32)


def head_masks():
    lane_head = lax.broadcasted_iota(jnp.int32, (WINDOW, WINDOW), 1) // HEAD_DIM
    return [jnp.where(lane_head == h, 1.0, 0.0).astype(BF) for h in range(4)]


class Window:
    def __init__(self, load, mask, store, spread):
        self.load, self.mask, self.store, self.spread = load, mask, store, spread

    def scores(self):
        q, k, v, d = self.load()
        self.keep = self.mask().astype(F32)
        self.q4 = jnp.concatenate([q * m for m in self.spread], 0)
        self.d4 = jnp.concatenate([d * m for m in self.spread], 0)
        self.s = mm_nt(k, self.q4)
        self.da = mm_nt(v, self.d4)
        self.k_t, self.v_t = k.T, v.T

    def softmax(self):
        low, dsc = [], []
        for h in range(4):
            cols = slice(h * WINDOW, (h + 1) * WINDOW)
            e = jnp.exp2(self.s[:, cols] * EXP2_SCALE) * self.keep
            a = e * (1.0 / jnp.sum(e, axis=0, keepdims=True))
            d = self.da[:, cols]
            center = jnp.sum(a * d, axis=0, keepdims=True)
            low.append(a.astype(BF))
            dsc.append((a * (d - center)).astype(BF))
        self.low = jnp.concatenate(low, 1)
        self.dsc = jnp.concatenate(dsc, 1)

    def outputs(self):
        ctx_t, dq_t = [], []
        for pair in range(2):
            rows = slice(pair * 64, pair * 64 + 64)
            cols = slice(pair * 256, pair * 256 + 256)
            c2 = mm(self.v_t[rows], self.low[:, cols])
            q2 = mm(self.k_t[rows], self.dsc[:, cols])
            ctx_t += [c2[:32, :128], c2[32:, 128:]]
            dq_t += [q2[:32, :128], q2[32:, 128:]]
        dv = mm(self.low, self.d4)
        dk = mm(self.dsc, self.q4) * SCALE
        ctx = jnp.concatenate(ctx_t, 0).T
        dq = jnp.concatenate(dq_t, 0).T * SCALE
        self.store((ctx, dq, dk, dv))


def build_weights(side, own_ref, oth_ref, wqkv, wqkv_t, wout_t, wout_p):
    for part in range(2):
        cols = slice(part * 64, part * 64 + 64)
        for j in range(3):
            in_rows = slice(j * 256, j * 256 + 256)
            wqkv[:, part * 384 + j * 128 : part * 384 + j * 128 + 128] = jnp.concatenate(
                [own_ref[in_rows, cols], oth_ref[in_rows, cols]], 1
            )
        for pos, half in enumerate((own_ref, oth_ref)):
            dst_rows = slice(part * 128 + pos * 64, part * 128 + pos * 64 + 64)
            for col in range(2):
                natural = half[768 + 128 * col + part * 64 : 768 + 128 * col + part * 64 + 64, :]
                wout_t[dst_rows, col * 128 : col * 128 + 128] = natural
                turn = jnp.where(side == 0, col, 1 - col)
                start = pl.multiple_of(768 + 128 * turn + part * 64, 64)
                wout_p[dst_rows, col * 128 : col * 128 + 128] = half[pl.ds(start, 64), :]
    wout_t[...] = wout_t[...].T
    wqkv_t[:, 0:128] = wqkv[pl.ds(pl.multiple_of(side * 128, 128), 128), :].T
    wqkv_t[:, 128:256] = wqkv[pl.ds(pl.multiple_of((1 - side) * 128, 128), 128), :].T


class Plan:
    def __init__(self, first_group, groups, first, last, beyond, send, got):
        self.first_group, self.groups = first_group, groups
        self.first, self.last, self.beyond, self.send = first, last, beyond, send
        self.got = got
        self.blocks = groups - (1 if first else 0)
        self.rows = self.blocks * GROUP


def chunk_kernel(plan, norm, *refs):
    refs = list(refs)
    take = lambda n: [refs.pop(0) for _ in range(n)]
    groups, first = plan.groups, plan.first
    grads_on = not plan.beyond
    counts_hbm, x_hbm, c_hbm = take(3)
    if first:
        halo_hbm, own_ref, oth_ref = take(3)
    else:
        weights_c = take(4)
        carry_c = take(3)
        gacc_c = take(1)[0] if grads_on else None
        take(2)
    got_hbm = take(1)[0] if plan.got else None
    out_full, gn_full = take(2)
    send = take(1)[0] if plan.send else None
    if first:
        weights = take(4)
    carry_n = take(3) if grads_on else None
    g_out = take(1)[0] if grads_on else None
    (xs, cs, near_in, near_out, far_out, far_stage, far_res, gacc, gacc_in, keep_o, keep_g, send_st, counts) = take(13)
    in_sems, misc_sems, out_sems = take(3)
    if not first:
        weights = take(4)
    if plan.got:
        got_st, got_sems = take(2)
    wqkv, wqkv_t, wout_t, wout_p = weights

    side = lax.axis_index("head").astype(jnp.int32)
    place = lax.axis_index(("gz", "tile")).astype(jnp.int32)
    total_blocks = counts.shape[0]
    slab = x_hbm.shape[0]
    width = xs.shape[1]
    up = GROUP * plan.first_group - GROUP
    down = slab - HALO - GROUP * (plan.first_group + groups - 1)
    origin = up + side * (down - up)
    first_block = place * (slab // WINDOW) + (origin + GROUP) // WINDOW - GROUP // WINDOW + total_blocks
    carry_in = pl.ds(pl.multiple_of(side * groups * GROUP, HALO), HALO)
    carry_out = pl.ds(pl.multiple_of((1 - side) * groups * GROUP, HALO), HALO)

    def count_of(row):
        return counts[lax.rem(first_block + row // WINDOW, total_blocks)]

    def piece_place(k):
        piece = k + side * (2 * groups - 2 * k)
        return piece, pl.ds(pl.multiple_of(piece * HALO, HALO), HALO)

    copies = [pltpu.make_async_copy(counts_hbm, counts, misc_sems.at[0])]
    if not first:
        for k in range(4):
            copies.append(pltpu.make_async_copy(weights_c[k], weights[k], misc_sems.at[1 + k]))
        for k, buffer in enumerate((near_in, near_out, far_out)):
            copies.append(pltpu.make_async_copy(carry_c[k], buffer.at[carry_in], misc_sems.at[5 + k]))
    for copy in copies:
        copy.start()
    for k in range(1 if first else 0, 2 * groups + 1):
        piece, dst = piece_place(k)
        if first and k == 1:
            pltpu.make_async_copy(halo_hbm.at[:, pl.ds(0, width)], xs.at[dst], in_sems.at[k, 0]).start()
            pltpu.make_async_copy(halo_hbm.at[:, pl.ds(width, width)], cs.at[dst], in_sems.at[k, 1]).start()
        else:
            src = pl.ds(pl.multiple_of(origin + piece * HALO, HALO), HALO)
            pltpu.make_async_copy(x_hbm.at[src], xs.at[dst], in_sems.at[k, 0]).start()
            pltpu.make_async_copy(c_hbm.at[src], cs.at[dst], in_sems.at[k, 1]).start()
    if plan.got:
        got_load = pltpu.make_async_copy(got_hbm, got_st, got_sems.at[2])
        got_load.start()
    if grads_on and not first:
        gacc_load = pltpu.make_async_copy(gacc_c, gacc_in, misc_sems.at[8])
        gacc_load.start()

    def wait_piece(k):
        _, dst = piece_place(k)
        pltpu.make_async_copy(x_hbm.at[pl.ds(0, HALO)], xs.at[dst], in_sems.at[k, 0]).wait()
        pltpu.make_async_copy(c_hbm.at[pl.ds(0, HALO)], cs.at[dst], in_sems.at[k, 1]).wait()

    row_iota = lax.broadcasted_iota(jnp.int32, (WINDOW, WINDOW), 0)
    wide_iota = lax.broadcasted_iota(jnp.int32, (WINDOW, 256), 0)

    def mask_cot(start):
        piece = pl.ds(pl.multiple_of(start, WINDOW), WINDOW)
        cs[piece, :] = jnp.where(wide_iota < count_of(start), cs[piece, :].astype(F32), 0.0).astype(BF)

    if first:
        build_weights(side, own_ref, oth_ref, wqkv, wqkv_t, wout_t, wout_p)
    if grads_on:
        gacc[...] = jnp.zeros_like(gacc)
    for copy in copies:
        copy.wait()
    if not first:
        wait_piece(0)
        for b in range(2):
            mask_cot(side * groups * GROUP + b * WINDOW)

    def base_of(i):
        return HALO + i * GROUP + side * (GROUP * groups - 3 * HALO - 2 * GROUP * i)

    def ready_of(base, part):
        return base - HALO + part * HALO + side * (3 * HALO - 2 * HALO * part)

    def result_copies(i):
        start = pl.multiple_of(ready_of(base_of(i), 0) - side * HALO, HALO)
        here = pl.ds(start, GROUP)
        final = pl.ds(pl.multiple_of(origin + start, HALO), GROUP)
        found = [
            pltpu.make_async_copy(keep_o.at[here], out_full.at[final], out_sems.at[i, 0]),
            pltpu.make_async_copy(keep_g.at[here], gn_full.at[final], out_sems.at[i, 1]),
        ]
        if plan.send:
            first_row = (1 - side) * (GROUP if first else 0) + side * HALO
            there = pl.ds(pl.multiple_of(start - first_row, HALO), GROUP)
            found.append(pltpu.make_async_copy(send_st.at[here], send.at[there], out_sems.at[i, 2]))
        return found

    def step(i, with_finish):
        base = pl.multiple_of(base_of(i), HALO)
        here = pl.ds(base, GROUP)
        wait_piece(2 * i + 1)
        wait_piece(2 * i + 2)
        for b in range(4):
            mask_cot(base + b * WINDOW)
        proj = mm(xs[here, :], wqkv[...])
        dctx = mm(cs[here, :], wout_t[...])
        near_in[here, 0:384] = proj[:, 0:384].astype(BF)
        near_in[here, 384:512] = dctx[:, 0:128].astype(BF)
        for j in range(3):
            far_stage[j] = proj[:, 384 + 128 * j : 512 + 128 * j]
        far_stage[3] = dctx[:, 128:256]
        spread = head_masks()

        def far_window(r):
            def load():
                return [far_stage[j, pl.ds(r, WINDOW, stride=4), :].astype(BF) for j in range(4)]

            def mask():
                quarter = row_iota // 32
                limit = jnp.where(
                    quarter < 2,
                    jnp.where(quarter == 0, count_of(base), count_of(base + WINDOW)),
                    jnp.where(quarter == 2, count_of(base + 2 * WINDOW), count_of(base + 3 * WINDOW)),
                )
                return 4 * (row_iota - 32 * quarter) + r < limit

            def store(result):
                for j in range(4):
                    far_res[j, pl.ds(r, WINDOW, stride=4), :] = result[j]

            return Window(load, mask, store, spread)

        def near_window(k):
            start = base - 64 + WINDOW * k + side * (WINDOW + WINDOW * (3 - 2 * k))
            spot = pl.ds(pl.multiple_of(start, 64), WINDOW)

            def load():
                block = near_in[spot, :]
                return [block[:, 128 * j : 128 * j + 128] for j in range(4)]

            def mask():
                limit = jnp.where(row_iota < 64, count_of(start - 64) - 64, count_of(start + 64) + 64)
                return row_iota < limit

            def store(result):
                for j in range(4):
                    near_out[spot, 128 * j : 128 * j + 128] = result[j].astype(BF)

            return Window(load, mask, store, spread)

        def finish(part):
            start = pl.multiple_of(ready_of(base, part), HALO)
            ready = pl.ds(start, HALO)
            near = near_out[ready, :]
            far = far_out[ready, :]
            ctx = jnp.concatenate([near[:, :128], far[:, :128]], 1)
            grads = jnp.concatenate([near[:, 128:], far[:, 128:]], 1)
            wp, wt = (wout_p, wqkv_t) if plan.send else (wout_p.at[:, pl.ds(0, 128)], wqkv_t.at[:, pl.ds(0, 128)])
            out = mm(ctx, wp[...])
            parts = []
            for q in range(2):
                rows = slice(q * WINDOW, (q + 1) * WINDOW)
                keep = wide_iota[:, : out.shape[1]] < count_of(start + q * WINDOW)
                parts.append(jnp.where(keep, out[rows], 0.0))
            out = jnp.concatenate(parts, 0).astype(BF)
            gn = mm(grads, wt[...]).astype(BF)
            keep_o[ready, :] = out[:, :128]
            keep_g[ready, :] = gn[:, :128]
            if plan.send:
                send_st[ready, 0:128] = out[:, 128:]
                send_st[ready, 128:256] = gn[:, 128:]
            if grads_on:
                gacc[:, 0:768] += mm(turned_x[part], grads)
                gacc[:, 768:1024] += mm(turned_c[part], ctx)

        if with_finish and grads_on:
            halves = [pl.ds(pl.multiple_of(ready_of(base, p), HALO), HALO) for p in range(2)]
            turned_x = [xs[half, :].T for half in halves]
            turned_c = [cs[half, :].T for half in halves]

        line = [near_window(0)] + [far_window(r) for r in range(4)] + [near_window(k) for k in range(1, 4)]
        count = len(line)
        for t in range(count + 2):
            if t < count:
                line[t].scores()
            if 1 <= t <= count:
                line[t - 1].softmax()
            if t >= 2:
                line[t - 2].outputs()
            if t == 3 and with_finish:
                finish(0)
            if t == 6:
                for j in range(4):
                    far_out[here, 128 * j : 128 * j + 128] = far_res[j].astype(BF)
        if with_finish:
            finish(1)
            for copy in result_copies(i):
                copy.start()

    start = 0
    if first:
        step(0, False)
        start = 1
    if plan.got:
        got_load.wait()
        row, size = plan.got
        theirs = side * row + (1 - side) * (slab - row - size)
        theirs = pl.ds(pl.multiple_of(theirs, HALO), size)
        got_copies = (
            pltpu.make_async_copy(got_st.at[:, pl.ds(0, 128)], out_full.at[theirs], got_sems.at[0]),
            pltpu.make_async_copy(got_st.at[:, pl.ds(128, 128)], gn_full.at[theirs], got_sems.at[1]),
        )
        for copy in got_copies:
            copy.start()

    def loop_body(i, _):
        step(i, True)
        return 0

    lax.fori_loop(start, groups, loop_body, 0)

    if grads_on:
        passed = [
            pltpu.make_async_copy(near_in.at[carry_out], carry_n[0], misc_sems.at[0]),
            pltpu.make_async_copy(near_out.at[carry_out], carry_n[1], misc_sems.at[1]),
            pltpu.make_async_copy(far_out.at[carry_out], carry_n[2], misc_sems.at[2]),
        ]
        for copy in passed:
            copy.start()
        if not first:
            gacc_load.wait()
            gacc[...] = gacc[...] + gacc_in[...]
        if plan.last:
            turned_out = gacc[:, 768:1024].T
            for pos in range(2):
                half = side if pos == 0 else 1 - side
                for j in range(3):
                    near = gacc[:, 128 * j + 64 * pos : 128 * j + 64 * pos + 64]
                    far = gacc[:, 384 + 128 * j + 64 * pos : 384 + 128 * j + 64 * pos + 64]
                    g_out[half, 256 * j : 256 * j + 256, :] = (jnp.concatenate([near, far], 1) * norm).astype(BF)
                for part in range(2):
                    for col in range(2):
                        rows = slice(128 * part + 64 * pos, 128 * part + 64 * pos + 64)
                        piece = turned_out[rows, 128 * col : 128 * col + 128]
                        low = 768 + 128 * col + 64 * part
                        g_out[half, low : low + 64, :] = (piece * norm).astype(BF)
        else:
            passed.append(pltpu.make_async_copy(gacc, g_out, misc_sems.at[3]))
            passed[-1].start()
        for copy in passed:
            copy.wait()
    for i in range(1 if first else 0, groups):
        for copy in result_copies(i):
            copy.wait()
    if plan.got:
        for copy in got_copies:
            copy.wait()


def chunk_call(plan, norm, counts, nodes_in, cotangent, halo, weights, carry, gacc, fulls, got):
    vmem = pl.BlockSpec(memory_space=pltpu.VMEM)
    hbm = pl.BlockSpec(memory_space=pl.ANY)
    slab = nodes_in.shape[0]
    groups, first, grads_on = plan.groups, plan.first, not plan.beyond
    buffer = HALO + groups * GROUP
    sds = jax.ShapeDtypeStruct
    weight_shapes = [(256, 768), (768, 256), (256, 256), (256, 256)]
    aliases = {}
    if first:
        args = [counts, nodes_in, cotangent, halo] + list(weights)
        in_specs = [hbm] * 4 + [vmem] * 2
    else:
        args = [counts, nodes_in, cotangent] + list(weights) + list(carry) + ([gacc] if grads_on else []) + list(fulls)
        in_specs = [hbm] * len(args)
        aliases = {len(args) - 2: 0, len(args) - 1: 1}
    if got is not None:
        args.append(got)
        in_specs.append(hbm)
    out_shape = [sds((slab, 128), BF), sds((slab, 128), BF)]
    if plan.send:
        out_shape.append(sds((plan.rows, 256), BF))
    out_specs = [hbm] * len(out_shape)
    if first:
        out_shape += [sds(shape, BF) for shape in weight_shapes]
        out_specs += [vmem] * 4
    if grads_on:
        out_shape += [sds((HALO, 512), BF)] * 3
        out_specs += [hbm] * 3
        out_shape.append(sds((2, 1024, 128), BF) if plan.last else sds((256, 1024), F32))
        out_specs.append(vmem if plan.last else hbm)
    scratch = [
        pltpu.VMEM((buffer, 256), BF),
        pltpu.VMEM((buffer, 256), BF),
        pltpu.VMEM((buffer, 512), BF),
        pltpu.VMEM((buffer, 512), BF),
        pltpu.VMEM((buffer, 512), BF),
        pltpu.VMEM((4, GROUP, 128), F32),
        pltpu.VMEM((4, GROUP, 128), F32),
        pltpu.VMEM((256, 1024), F32),
        pltpu.VMEM((256, 1024), F32),
        pltpu.VMEM((buffer, 128), BF),
        pltpu.VMEM((buffer, 128), BF),
        pltpu.VMEM((buffer, 256), BF),
        pltpu.SMEM((counts.shape[0],), jnp.int32),
        pltpu.SemaphoreType.DMA((2 * groups + 1, 2)),
        pltpu.SemaphoreType.DMA((9,)),
        pltpu.SemaphoreType.DMA((groups, 3)),
    ]
    if not first:
        scratch += [pltpu.VMEM(shape, BF) for shape in weight_shapes]
    if got is not None:
        scratch += [pltpu.VMEM(got.shape, BF), pltpu.SemaphoreType.DMA((3,))]
    outs = pl.pallas_call(
        functools.partial(chunk_kernel, plan, norm),
        out_shape=out_shape,
        in_specs=in_specs,
        out_specs=out_specs,
        input_output_aliases=aliases,
        scratch_shapes=scratch,
        compiler_params=pltpu.CompilerParams(vmem_limit_bytes=VMEM_LIMIT),
        cost_estimate=pl.CostEstimate(
            flops=plan.rows * 4000000, bytes_accessed=plan.rows * 3000, transcendentals=0
        ),
    )(*args)
    outs = list(outs)
    fulls, rest = outs[:2], outs[2:]
    sent = rest.pop(0) if plan.send else None
    if first:
        weights, rest = rest[:4], rest[4:]
    if grads_on:
        carry, gacc = rest[:3], rest[3]
    return fulls, sent, weights, carry, gacc


def pack_kernel(x_hbm, c_hbm, wq, wk, wv, wo, packed, rims, sems):
    side = lax.axis_index("head").astype(jnp.int32)
    rows = pl.ds(pl.multiple_of((1 - side) * (x_hbm.shape[0] - HALO), HALO), HALO)
    copies = (
        pltpu.make_async_copy(x_hbm.at[rows], rims.at[:, pl.ds(0, 256)], sems.at[0]),
        pltpu.make_async_copy(c_hbm.at[rows], rims.at[:, pl.ds(256, 256)], sems.at[1]),
    )
    for copy in copies:
        copy.start()
    packed[0:256, :] = wq[...]
    packed[256:512, :] = wk[...]
    packed[512:768, :] = wv[...]
    packed[768:896, :] = wo[:, 0:128]
    packed[896:1024, :] = wo[:, 128:256]
    for copy in copies:
        copy.wait()


def pack_call(nodes_in, cotangent, w_query, w_key, w_value, w_out):
    vmem = pl.BlockSpec(memory_space=pltpu.VMEM)
    hbm = pl.BlockSpec(memory_space=pl.ANY)
    return pl.pallas_call(
        pack_kernel,
        out_shape=(jax.ShapeDtypeStruct((1024, 128), BF), jax.ShapeDtypeStruct((HALO, 512), BF)),
        in_specs=[hbm, hbm, vmem, vmem, vmem, vmem],
        out_specs=(vmem, vmem),
        scratch_shapes=[pltpu.SemaphoreType.DMA((2,))],
    )(nodes_in, cotangent, w_query, w_key, w_value, w_out)


def per_device(nodes_in, cotangent, w_query, w_key, w_value, w_out, counts):
    row_count = nodes_in.shape[0]
    gz, heads, tiles = lax.axis_size("gz"), lax.axis_size("head"), lax.axis_size("tile")
    places = gz * tiles
    swap = [(0, 1), (1, 0)]

    def flat(p, h):
        return (p // tiles * heads + h) * tiles + p % tiles

    own, rims = pack_call(nodes_in, cotangent, w_query, w_key, w_value, w_out)
    oth = lax.ppermute(own, "head", swap)
    route = [(flat(p, 0), flat((p + 1) % places, 0)) for p in range(places)]
    route += [(flat(p, 1), flat((p - 1) % places, 1)) for p in range(places)]
    halo = lax.ppermute(rims, ("gz", "head", "tile"), route)

    norm = float(row_count * places) ** (-0.5)
    weights, carry, gacc, fulls = (own, oth), None, None, None
    waiting, first_group, row = [], 0, 0
    for n, groups in enumerate(CALL_GROUPS + (BEYOND,)):
        first, beyond = n == 0, n == len(CALL_GROUPS)
        last = n == len(CALL_GROUPS) - 1
        send = not last and not beyond
        got_rows, got = waiting.pop(0) if len(waiting) > (0 if beyond else 1) else (None, None)
        spot = None if got is None else (got_rows, got.shape[0])
        plan = Plan(first_group, groups, first, last, beyond, send, spot)
        fulls, sent, weights, carry, gacc = chunk_call(
            plan, norm, counts, nodes_in, cotangent, halo, weights, carry, gacc, fulls, got
        )
        if send:
            waiting.append((row, lax.ppermute(sent, "head", swap)))
        first_group += groups
        row += plan.rows

    part = 1024 // places
    grads = gacc.reshape(heads * places, part, 128)
    grads = lax.all_to_all(grads, ("head", "gz", "tile"), 0, 0, tiled=True)
    share = jnp.sum(grads.astype(F32), axis=0).astype(BF)
    share, *fulls = lax.optimization_barrier((share, *fulls))
    share = jnp.broadcast_to(share[None], (places,) + share.shape)
    whole = lax.all_to_all(share, ("gz", "tile"), 0, 0, tiled=True).reshape(1024, 128).astype(F32)
    grad_out = jnp.concatenate([whole[768:896], whole[896:1024]], 1)
    return (fulls[0], fulls[1], whole[0:256], whole[256:512], whole[512:768], grad_out)


def solution(mesh):
    return jax.shard_map(
        per_device,
        mesh=mesh,
        in_specs=(
            P(("gz", "tile"), None),
            P(("gz", "tile"), None),
            P(None, "head"),
            P(None, "head"),
            P(None, "head"),
            P("head", None),
            P(),
        ),
        out_specs=(
            P(("gz", "tile"), "head"),
            P(("gz", "tile"), "head"),
            P(None, "head"),
            P(None, "head"),
            P(None, "head"),
            P("head", None),
        ),
        check_vma=False,
    )
```

time: 878 us -> 104 us (0.12)
  waiting for transfers between devices: 530 us -> 6.94 us
  local copies, waits for them, and re-layouts: 204 us -> 3.43 us
  matrix products: 92.7 us -> 0 us
  Pallas kernels: 0 us -> 54.1 us
  other arithmetic: 22.2 us -> 0.81 us
  blocking collectives: 0 us -> 18.5 us
  between operations: 16.4 us -> 0.72 us
  starting transfers between devices: 4.61 us -> 18.2 us
    psum x1 -> x0, waiting for transfers between devices: 526 us -> none  [per_device(): lax.psum((grad_query, grad_key, grad_value, grad_out), ('gz', 'tile'))]
    reshape x16 -> x0, local copies, waits for them, and re-layouts: 97.3 us -> none  [the longest x8 36.9 us: to_windows(): array.reshape(length // (WINDOW * dilation), WINDOW, dilation, head_count...]
    dot_general x24 -> x0, matrix products: 92.7 us -> none  [the longest x2 8.5 us: window_core(): jnp.einsum('whqk,whqe->whke', attention_low, dcontext, preferred_element_...]
    pallas_call x0 -> x5, Pallas kernels: none -> 54.1 us  [the longest x4 51.3 us: chunk_call(): pl.pallas_call(functools.partial(chunk_kernel, plan, norm), out_shape=out...]
    transpose x8 -> x0, local copies, waits for them, and re-layouts: 43.7 us -> none  [the longest x4 40.9 us: to_windows(): shaped.transpose(0, 2, 3, 1, 4).reshape(-1, head_count, WINDOW, head_dim)]
    unnamed x84 -> x8, local copies, waits for them, and re-layouts: 33.9 us -> 2.63 us
    slice x27 -> x2, local copies, waits for them, and re-layouts: 26.7 us -> 0.76 us  [the longest x1 0.75 us: per_device(): whole[512:768]]
    all_to_all x0 -> x1, blocking collectives: none -> 18.5 us  [per_device(): lax.all_to_all(share, ('gz', 'tile'), 0, 0, tiled=True).reshape(1024, 128)]
  transfers between devices with their start and end apart: 5 -> 5, of which waited for: 3 -> 2; matrix products, arithmetic and copies ran while one was open for 4% -> 0% of each run, Pallas kernels for 0% -> 37%
where the time goes in v2:
time: 104 us; the launch traced here: 103 us
  Pallas kernels  54.1 us (52%)
  blocking collectives  18.5 us (18%)
  starting transfers between devices  18.2 us (18%)
  waiting for transfers between devices  6.94 us (7%)
  local copies, waits for them, and re-layouts  3.43 us (3%)
    pallas_call x4, Pallas kernels, chunk_call(): pl.pallas_call(functools.partial(chunk_kernel, plan, norm), out_shape=out...  51.3 us
    all_to_all x1, blocking collectives, per_device(): lax.all_to_all(share, ('gz', 'tile'), 0, 0, tiled=True).reshape(1024, 128)  18.5 us
    all_to_all x1, starting transfers between devices, per_device(): grads = lax.all_to_all(grads, ('head', 'gz', 'tile'), 0, 0, tiled=True)  10.5 us
    ppermute x1, waiting for transfers between devices, per_device(): halo = lax.ppermute(rims, ('gz', 'head', 'tile'), route)  6.44 us
    ppermute x1, starting transfers between devices, per_device(): halo = lax.ppermute(rims, ('gz', 'head', 'tile'), route)  4.4 us
    ppermute x2, starting transfers between devices, per_device(): waiting.append((row, lax.ppermute(sent, 'head', swap)))  3.31 us
    pallas_call x1, Pallas kernels, pack_call(): pl.pallas_call(pack_kernel, out_shape=(jax.ShapeDtypeStruct((1024, 128),...  2.72 us
    unnamed x8, local copies, waits for them, and re-layouts  2.63 us
  transfers between devices with their start and end apart: 5, of which 2 were waited for; matrix products, arithmetic and copies ran while one was open for 0% of the time, Pallas kernels for 37%

profile of v2, /device:TPU:17, one launch (start us, length us, event | category | flops | bytes accessed | tf_op | source)
XLA Modules:
  0.0 102.6 jit_solution(2402473072366823772)
XLA Ops:
  0.6 2.7 %shard_map.118 = (bf16[1024,128]{1,0:T(8,128)(2,1)}, bf16[256,512]{1,0:T(8,128)(2,1)}) custom-call(bf16[8192,256]{1,0:T(8,128)(2,1)} %refs_1_.7, bf16[8192,256]{1,0:T(8,128)(2,1)} %refs_2_.7, bf16[256,128]{1,0:T(8,128)(2,1)} %wq.1, bf16[256,128]{1,0:T(8,128)(2,1)} %wk.1, bf16[256,128]{1,0:T(8,128)(2,1)} %wv.1, bf16[128,256]{1,0:T(8,128)(2,1)} %wo.1), custom_call_target="tpu_custom_call" | custom-call | tf_op jit(solution)/shard_map/pallas_call | solution.py:481
  3.4 4.4 %collective-permute-start = (bf16[256,512]{1,0:T(8,128)(2,1)}, bf16[256,512]{1,0:T(8,128)(2,1)S(1)}, u32[]{:S(2)}, u32[]{:S(2)}) collective-permute-start(bf16[256,512]{1,0:T(8,128)(2,1)} %get-tuple-element.37), channel_id=1, source_target_pairs={{0,1},{1,2},{2,3},{3,8},{8,9},{9,10},{10,11},{11,16},{16,17},{17,1... | collective-permute-start | bytes 786440 | tf_op jit(solution)/shard_map/ppermute | solution.py:503
  7.8 0.0 collective-permute-start.1
  7.8 6.4 %collective-permute-done.refs_3_ = bf16[256,512]{1,0:T(8,128)(2,1)S(1)} collective-permute-done((bf16[256,512]{1,0:T(8,128)(2,1)}, bf16[256,512]{1,0:T(8,128)(2,1)S(1)}, u32[]{:S(2)}, u32[]{:S(2)}) %collective-permute-start) | collective-permute-done | bytes 262176 | tf_op jit(solution)/shard_map/ppermute | solution.py:503
  14.2 0.0 copy-start.2
  14.2 0.5 collective-permute-done.1.refs_5_
  14.7 0.2 copy-done.2
  14.9 0.0 copy-start.3
  14.9 0.7 copy-done.3
  15.6 13.5 %shard_map.119 = (bf16[8192,128]{1,0:T(8,128)(2,1)}, bf16[8192,128]{1,0:T(8,128)(2,1)}, bf16[1024,256]{1,0:T(8,128)(2,1)}, bf16[256,768]{1,0:T(8,128)(2,1)}, bf1...) custom-call(s32[4096]{0:T(1024)} %refs_0_.7, ...), custom_call_target="tpu_custom_call" | custom-call | flops 4096000000 | bytes 3072000 | tf_op jit(solution)/shard_map/pallas_call | solution.py:438
  29.2 1.1 %collective-permute-start.2 = (bf16[1024,256]{1,0:T(8,128)(2,1)}, bf16[1024,256]{1,0:T(8,128)(2,1)S(1)}, u32[]{:S(2)}, u32[]{:S(2)}) collective-permute-start(bf16[1024,256]{1,0:T(8,128)(2,1)} %get-tuple-element.55), channel_id=1, source_target_pairs={{0,4},{4,0},{1,5},{5,1},{2,6},{6,2},{3,7},{7,3},{8,12},{12,8},{9,1... | collective-permute-start | bytes 1572872 | tf_op jit(solution)/shard_map/ppermute | solution.py:519
  30.2 12.7 %shard_map.120 = (bf16[8192,128]{1,0:T(8,128)(2,1)}, bf16[8192,128]{1,0:T(8,128)(2,1)}, bf16[1536,256]{1,0:T(8,128)(2,1)}, bf16[256,512]{1,0:T(8,128)(2,1)}, bf1...) custom-call(s32[4096]{0:T(1024)} %refs_0_.7, ...), custom_call_target="tpu_custom_call", output_to_operand_aliasing={{0}: (11, {}), {1}: (12, {})} | custom-call | flops 6144000000 | bytes 4608000 | tf_op jit(solution)/shard_map/pallas_call | solution.py:438
  43.0 2.3 %collective-permute-start.3 = (bf16[1536,256]{1,0:T(8,128)(2,1)}, bf16[1536,256]{1,0:T(8,128)(2,1)S(1)}, u32[]{:S(2)}, u32[]{:S(2)}) collective-permute-start(bf16[1536,256]{1,0:T(8,128)(2,1)} %get-tuple-element.62), channel_id=1, source_target_pairs={{0,4},{4,0},{1,5},{5,1},{2,6},{6,2},{3,7},{7,3},{8,12},{12,8},{9,1... | collective-permute-start | bytes 2359304 | tf_op jit(solution)/shard_map/ppermute | solution.py:519
  45.2 0.0 collective-permute-done.2.refs_13_
  45.2 0.0 copy-start.1
  45.2 0.8 copy-done.1
  46.0 13.4 %shard_map.121 = (bf16[8192,128]{1,0:T(8,128)(2,1)}, bf16[8192,128]{1,0:T(8,128)(2,1)}, bf16[256,512]{1,0:T(8,128)(2,1)}, bf16[256,512]{1,0:T(8,128)(2,1)}, bf16...) custom-call(s32[4096]{0:T(1024)} %refs_0_.7, ...), custom_call_target="tpu_custom_call", output_to_operand_aliasing={{0}: (11, {}), {1}: (12, {})} | custom-call | flops 6144000000 | bytes 4608000 | tf_op jit(solution)/shard_map/pallas_call | solution.py:438
  59.4 10.5 %all-to-all-start = ((bf16[128,16,128]{2,1,0:T(8,128)(2,1)}), bf16[128,16,128]{2,1,0:T(8,128)(2,1)S(1)}, u32[]{:S(2)}, u32[]{:S(2)}) async-start(bf16[128,16,128]{2,1,0:T(8,128)(2,1)} %bitcast.6), calls=%async_computation | async-start | bytes 1048576 | tf_op jit(solution)/shard_map/all_to_all | solution.py:525
  69.9 0.0 collective-permute-done.3.refs_12_
  69.9 0.0 copy-start
  69.9 0.9 copy-done
  70.8 11.7 %shard_map.122 = (bf16[8192,128]{1,0:T(8,128)(2,1)}, bf16[8192,128]{1,0:T(8,128)(2,1)}) custom-call(s32[4096]{0:T(1024)} %refs_0_.7, bf16[8192,256]{1,0:T(8,128)(2,1)} %refs_1_.7, bf16[8192,256]{1,0:T(8,128)(2,1)} %refs_2_.7, bf16[256,768]{1,0:T(8,128)(2,1)} %get-tuple-element.39.refs_3_, ...), custom_call_target="tpu_custom_call", output_to_operand_aliasing={{0}: (10, {}), {1}: (11, {})} | custom-call | flops 6144000000 | bytes 4608000 | tf_op jit(solution)/shard_map/pallas_call | solution.py:438
  82.5 0.0 all-to-all-done
  82.5 0.1 reduce_sum.12
  82.7 18.5 %all_to_all.10 = bf16[64,16,128]{2,1,0:T(8,128)(2,1)S(1)} all-to-all(bf16[64,16,128]{2,1,0:T(8,128)(2,1)S(1)} %broadcast_in_dim.2), channel_id=1, replica_groups=mesh['gz'=16,'head'=2,'tile'=4] {'gz','tile'}, dimensions={0} | all-to-all | bytes 524288 | tf_op jit(solution)/shard_map/all_to_all | solution.py:529
  101.2 0.7 pad_maximum_fusion
  101.8 0.8 fusion.1
  (2 shorter events, 0.0 us)
Async XLA Ops:
  3.4 10.8 %collective-permute-start = (bf16[256,512]{1,0:T(8,128)(2,1)}, bf16[256,512]{1,0:T(8,128)(2,1)S(1)}, u32[]{:S(2)}, u32[]{:S(2)}) collective-permute-start(bf16[256,512]{1,0:T(8,128)(2,1)} %get-tuple-element.37), channel_id=1, source_target_pairs={{0,1},{1,2},{2,3},{3,8},{8,9},{9,10},{10,11},{11,16},{16,17},{17,1... | collective-permute-start | bytes 786440 | tf_op jit(solution)/shard_map/ppermute | solution.py:503
  7.8 6.9 %collective-permute-start.1 = (bf16[1024,128]{1,0:T(8,128)(2,1)}, bf16[1024,128]{1,0:T(8,128)(2,1)S(1)}, u32[]{:S(2)}, u32[]{:S(2)}) collective-permute-start(bf16[1024,128]{1,0:T(8,128)(2,1)} %get-tuple-element.38.refs_4_), channel_id=1, source_target_pairs={{0,4},{4,0},{1,5},{5,1},{2,6},{6,2},{3,7},{7,3},{8,12},{12,8},{9,1... | collective-permute-start | bytes 786440 | tf_op jit(solution)/shard_map/ppermute | solution.py:500
  14.2 0.7 copy-start.2
  14.9 0.7 copy-start.3
  29.2 16.1 %collective-permute-start.2 = (bf16[1024,256]{1,0:T(8,128)(2,1)}, bf16[1024,256]{1,0:T(8,128)(2,1)S(1)}, u32[]{:S(2)}, u32[]{:S(2)}) collective-permute-start(bf16[1024,256]{1,0:T(8,128)(2,1)} %get-tuple-element.55), channel_id=1, source_target_pairs={{0,4},{4,0},{1,5},{5,1},{2,6},{6,2},{3,7},{7,3},{8,12},{12,8},{9,1... | collective-permute-start | bytes 1572872 | tf_op jit(solution)/shard_map/ppermute | solution.py:519
  43.0 26.9 %collective-permute-start.3 = (bf16[1536,256]{1,0:T(8,128)(2,1)}, bf16[1536,256]{1,0:T(8,128)(2,1)S(1)}, u32[]{:S(2)}, u32[]{:S(2)}) collective-permute-start(bf16[1536,256]{1,0:T(8,128)(2,1)} %get-tuple-element.62), channel_id=1, source_target_pairs={{0,4},{4,0},{1,5},{5,1},{2,6},{6,2},{3,7},{7,3},{8,12},{12,8},{9,1... | collective-permute-start | bytes 2359304 | tf_op jit(solution)/shard_map/ppermute | solution.py:519
  45.2 0.8 copy-start.1
  59.4 23.1 %all-to-all-start = ((bf16[128,16,128]{2,1,0:T(8,128)(2,1)}), bf16[128,16,128]{2,1,0:T(8,128)(2,1)S(1)}, u32[]{:S(2)}, u32[]{:S(2)}) async-start(bf16[128,16,128]{2,1,0:T(8,128)(2,1)} %bitcast.6), calls=%async_computation | async-start | bytes 1048576 | tf_op jit(solution)/shard_map/all_to_all | solution.py:525
  69.9 0.9 copy-start

commit v3 on v2

--- a/solution.py
+++ b/solution.py
@@ -12,11 +12,11 @@
 HALO = 256
 GROUP = 512
 HEAD_DIM = 32
-CALL_GROUPS = (3, 3, 3)
-BEYOND = 3
+OWN_CALLS = (4, 5)
+BEYOND_CALLS = (3, 2)
 SCALE = HEAD_DIM ** (-0.5)
 EXP2_SCALE = SCALE * math.log2(math.e)
-VMEM_LIMIT = 56 * 1024 * 1024
+VMEM_LIMIT = 58 * 1024 * 1024
 BF = jnp.bfloat16
 F32 = jnp.float32
 
@@ -98,11 +98,13 @@
 
 
 class Plan:
-    def __init__(self, first_group, groups, first, last, beyond, send, got):
+    def __init__(self, first_group, groups, first, last, beyond, send, carry, got):
         self.first_group, self.groups = first_group, groups
         self.first, self.last, self.beyond, self.send = first, last, beyond, send
+        self.carry = carry
         self.got = got
         self.blocks = groups - (1 if first else 0)
+        self.cost = 200000 if beyond else 4000000
         self.rows = self.blocks * GROUP
 
 
@@ -113,7 +115,7 @@
     grads_on = not plan.beyond
     counts_hbm, x_hbm, c_hbm = take(3)
     if first:
-        halo_hbm, own_ref, oth_ref = take(3)
+        halo_hbm, own_hbm, oth_hbm = take(3)
     else:
         weights_c = take(4)
         carry_c = take(3)
@@ -124,11 +126,13 @@
     send = take(1)[0] if plan.send else None
     if first:
         weights = take(4)
-    carry_n = take(3) if grads_on else None
+    carry_n = take(3) if plan.carry else None
     g_out = take(1)[0] if grads_on else None
     (xs, cs, near_in, near_out, far_out, far_stage, far_res, gacc, gacc_in, keep_o, keep_g, send_st, counts) = take(13)
     in_sems, misc_sems, out_sems = take(3)
-    if not first:
+    if first:
+        own_ref, oth_ref = take(2)
+    else:
         weights = take(4)
     if plan.got:
         got_st, got_sems = take(2)
@@ -138,7 +142,6 @@
     place = lax.axis_index(("gz", "tile")).astype(jnp.int32)
     total_blocks = counts.shape[0]
     slab = x_hbm.shape[0]
-    width = xs.shape[1]
     up = GROUP * plan.first_group - GROUP
     down = slab - HALO - GROUP * (plan.first_group + groups - 1)
     origin = up + side * (down - up)
@@ -154,7 +157,10 @@
         return piece, pl.ds(pl.multiple_of(piece * HALO, HALO), HALO)
 
     copies = [pltpu.make_async_copy(counts_hbm, counts, misc_sems.at[0])]
-    if not first:
+    if first:
+        copies.append(pltpu.make_async_copy(own_hbm, own_ref, misc_sems.at[1]))
+        copies.append(pltpu.make_async_copy(oth_hbm, oth_ref, misc_sems.at[2]))
+    else:
         for k in range(4):
             copies.append(pltpu.make_async_copy(weights_c[k], weights[k], misc_sems.at[1 + k]))
         for k, buffer in enumerate((near_in, near_out, far_out)):
@@ -164,8 +170,8 @@
     for k in range(1 if first else 0, 2 * groups + 1):
         piece, dst = piece_place(k)
         if first and k == 1:
-            pltpu.make_async_copy(halo_hbm.at[:, pl.ds(0, width)], xs.at[dst], in_sems.at[k, 0]).start()
-            pltpu.make_async_copy(halo_hbm.at[:, pl.ds(width, width)], cs.at[dst], in_sems.at[k, 1]).start()
+            pltpu.make_async_copy(halo_hbm.at[:, pl.ds(0, 256)], xs.at[dst], in_sems.at[k, 0]).start()
+            pltpu.make_async_copy(halo_hbm.at[:, pl.ds(256, 256)], cs.at[dst], in_sems.at[k, 1]).start()
         else:
             src = pl.ds(pl.multiple_of(origin + piece * HALO, HALO), HALO)
             pltpu.make_async_copy(x_hbm.at[src], xs.at[dst], in_sems.at[k, 0]).start()
@@ -189,12 +195,12 @@
         piece = pl.ds(pl.multiple_of(start, WINDOW), WINDOW)
         cs[piece, :] = jnp.where(wide_iota < count_of(start), cs[piece, :].astype(F32), 0.0).astype(BF)
 
-    if first:
-        build_weights(side, own_ref, oth_ref, wqkv, wqkv_t, wout_t, wout_p)
     if grads_on:
         gacc[...] = jnp.zeros_like(gacc)
     for copy in copies:
         copy.wait()
+    if first:
+        build_weights(side, own_ref, oth_ref, wqkv, wqkv_t, wout_t, wout_p)
     if not first:
         wait_piece(0)
         for b in range(2):
@@ -344,14 +350,12 @@
 
     lax.fori_loop(start, groups, loop_body, 0)
 
+    passed = []
+    if plan.carry:
+        for k, buffer in enumerate((near_in, near_out, far_out)):
+            passed.append(pltpu.make_async_copy(buffer.at[carry_out], carry_n[k], misc_sems.at[k]))
+            passed[-1].start()
     if grads_on:
-        passed = [
-            pltpu.make_async_copy(near_in.at[carry_out], carry_n[0], misc_sems.at[0]),
-            pltpu.make_async_copy(near_out.at[carry_out], carry_n[1], misc_sems.at[1]),
-            pltpu.make_async_copy(far_out.at[carry_out], carry_n[2], misc_sems.at[2]),
-        ]
-        for copy in passed:
-            copy.start()
         if not first:
             gacc_load.wait()
             gacc[...] = gacc[...] + gacc_in[...]
@@ -363,17 +367,15 @@
                     near = gacc[:, 128 * j + 64 * pos : 128 * j + 64 * pos + 64]
                     far = gacc[:, 384 + 128 * j + 64 * pos : 384 + 128 * j + 64 * pos + 64]
                     g_out[half, 256 * j : 256 * j + 256, :] = (jnp.concatenate([near, far], 1) * norm).astype(BF)
-                for part in range(2):
-                    for col in range(2):
-                        rows = slice(128 * part + 64 * pos, 128 * part + 64 * pos + 64)
-                        piece = turned_out[rows, 128 * col : 128 * col + 128]
-                        low = 768 + 128 * col + 64 * part
-                        g_out[half, low : low + 64, :] = (piece * norm).astype(BF)
+                rows = [turned_out[128 * part + 64 * pos : 128 * part + 64 * pos + 64] for part in range(2)]
+                rows = jnp.concatenate(rows, 0).reshape(16, 8, 256)
+                rows = jnp.concatenate([rows[:, :, :128], rows[:, :, 128:]], 1).reshape(256, 128)
+                g_out[half, 768:1024, :] = (rows * norm).astype(BF)
         else:
             passed.append(pltpu.make_async_copy(gacc, g_out, misc_sems.at[3]))
             passed[-1].start()
-        for copy in passed:
-            copy.wait()
+    for copy in passed:
+        copy.wait()
     for i in range(1 if first else 0, groups):
         for copy in result_copies(i):
             copy.wait()
@@ -384,7 +386,8 @@
 
 def chunk_call(plan, norm, counts, nodes_in, cotangent, halo, weights, carry, gacc, fulls, got):
     vmem = pl.BlockSpec(memory_space=pltpu.VMEM)
-    hbm = pl.BlockSpec(memory_space=pl.ANY)
+    hbm = pl.BlockSpec(memory_space=pltpu.HBM)
+    either = pl.BlockSpec(memory_space=pl.ANY)
     slab = nodes_in.shape[0]
     groups, first, grads_on = plan.groups, plan.first, not plan.beyond
     buffer = HALO + groups * GROUP
@@ -393,26 +396,27 @@
     aliases = {}
     if first:
         args = [counts, nodes_in, cotangent, halo] + list(weights)
-        in_specs = [hbm] * 4 + [vmem] * 2
+        in_specs = [hbm] * 3 + [either] * 3
     else:
         args = [counts, nodes_in, cotangent] + list(weights) + list(carry) + ([gacc] if grads_on else []) + list(fulls)
-        in_specs = [hbm] * len(args)
+        in_specs = [hbm] * 3 + [either] * (len(args) - 5) + [hbm] * 2
         aliases = {len(args) - 2: 0, len(args) - 1: 1}
     if got is not None:
         args.append(got)
-        in_specs.append(hbm)
+        in_specs.append(either)
     out_shape = [sds((slab, 128), BF), sds((slab, 128), BF)]
     if plan.send:
         out_shape.append(sds((plan.rows, 256), BF))
-    out_specs = [hbm] * len(out_shape)
+    out_specs = [hbm] * 2 + [either] * (len(out_shape) - 2)
     if first:
         out_shape += [sds(shape, BF) for shape in weight_shapes]
         out_specs += [vmem] * 4
+    if plan.carry:
+        out_shape += [sds((HALO, 512), BF)] * 3
+        out_specs += [either] * 3
     if grads_on:
-        out_shape += [sds((HALO, 512), BF)] * 3
-        out_specs += [hbm] * 3
         out_shape.append(sds((2, 1024, 128), BF) if plan.last else sds((256, 1024), F32))
-        out_specs.append(vmem if plan.last else hbm)
+        out_specs.append(vmem if plan.last else either)
     scratch = [
         pltpu.VMEM((buffer, 256), BF),
         pltpu.VMEM((buffer, 256), BF),
@@ -431,7 +435,9 @@
         pltpu.SemaphoreType.DMA((9,)),
         pltpu.SemaphoreType.DMA((groups, 3)),
     ]
-    if not first:
+    if first:
+        scratch += [pltpu.VMEM((1024, 128), BF)] * 2
+    else:
         scratch += [pltpu.VMEM(shape, BF) for shape in weight_shapes]
     if got is not None:
         scratch += [pltpu.VMEM(got.shape, BF), pltpu.SemaphoreType.DMA((3,))]
@@ -444,7 +450,7 @@
         scratch_shapes=scratch,
         compiler_params=pltpu.CompilerParams(vmem_limit_bytes=VMEM_LIMIT),
         cost_estimate=pl.CostEstimate(
-            flops=plan.rows * 4000000, bytes_accessed=plan.rows * 3000, transcendentals=0
+            flops=plan.rows * plan.cost, bytes_accessed=plan.rows * 1000, transcendentals=0
         ),
     )(*args)
     outs = list(outs)
@@ -452,38 +458,39 @@
     sent = rest.pop(0) if plan.send else None
     if first:
         weights, rest = rest[:4], rest[4:]
-    if grads_on:
-        carry, gacc = rest[:3], rest[3]
+    carry, rest = (rest[:3], rest[3:]) if plan.carry else (None, rest)
+    gacc = rest[0] if grads_on else None
     return fulls, sent, weights, carry, gacc
 
 
-def pack_kernel(x_hbm, c_hbm, wq, wk, wv, wo, packed, rims, sems):
+def pack_kernel(x_hbm, c_hbm, wq, wk, wv, wo, packed, rims, stage, sems):
     side = lax.axis_index("head").astype(jnp.int32)
     rows = pl.ds(pl.multiple_of((1 - side) * (x_hbm.shape[0] - HALO), HALO), HALO)
-    copies = (
+    loads = [
         pltpu.make_async_copy(x_hbm.at[rows], rims.at[:, pl.ds(0, 256)], sems.at[0]),
         pltpu.make_async_copy(c_hbm.at[rows], rims.at[:, pl.ds(256, 256)], sems.at[1]),
-    )
-    for copy in copies:
+        pltpu.make_async_copy(wq, packed.at[pl.ds(0, 256)], sems.at[2]),
+        pltpu.make_async_copy(wk, packed.at[pl.ds(256, 256)], sems.at[3]),
+        pltpu.make_async_copy(wv, packed.at[pl.ds(512, 256)], sems.at[4]),
+        pltpu.make_async_copy(wo, stage, sems.at[5]),
+    ]
+    for copy in loads:
         copy.start()
-    packed[0:256, :] = wq[...]
-    packed[256:512, :] = wk[...]
-    packed[512:768, :] = wv[...]
-    packed[768:896, :] = wo[:, 0:128]
-    packed[896:1024, :] = wo[:, 128:256]
-    for copy in copies:
+    for copy in loads:
         copy.wait()
+    packed[768:896, :] = stage[:, 0:128]
+    packed[896:1024, :] = stage[:, 128:256]
 
 
 def pack_call(nodes_in, cotangent, w_query, w_key, w_value, w_out):
     vmem = pl.BlockSpec(memory_space=pltpu.VMEM)
-    hbm = pl.BlockSpec(memory_space=pl.ANY)
+    hbm = pl.BlockSpec(memory_space=pltpu.HBM)
     return pl.pallas_call(
         pack_kernel,
         out_shape=(jax.ShapeDtypeStruct((1024, 128), BF), jax.ShapeDtypeStruct((HALO, 512), BF)),
-        in_specs=[hbm, hbm, vmem, vmem, vmem, vmem],
+        in_specs=[hbm] * 6,
         out_specs=(vmem, vmem),
-        scratch_shapes=[pltpu.SemaphoreType.DMA((2,))],
+        scratch_shapes=[pltpu.VMEM(w_out.shape, BF), pltpu.SemaphoreType.DMA((6,))],
     )(nodes_in, cotangent, w_query, w_key, w_value, w_out)
 
 
@@ -505,29 +512,32 @@
     norm = float(row_count * places) ** (-0.5)
     weights, carry, gacc, fulls = (own, oth), None, None, None
     waiting, first_group, row = [], 0, 0
-    for n, groups in enumerate(CALL_GROUPS + (BEYOND,)):
-        first, beyond = n == 0, n == len(CALL_GROUPS)
-        last = n == len(CALL_GROUPS) - 1
-        send = not last and not beyond
-        got_rows, got = waiting.pop(0) if len(waiting) > (0 if beyond else 1) else (None, None)
+    own_count, beyond_count = len(OWN_CALLS), len(BEYOND_CALLS)
+
+    for n, groups in enumerate(OWN_CALLS + BEYOND_CALLS):
+        first, beyond = n == 0, n >= own_count
+        last, end = n == own_count - 1, n == own_count + beyond_count - 1
+        send = n < own_count - 1
+        got_rows, got = waiting.pop(0) if waiting and n > 1 else (None, None)
         spot = None if got is None else (got_rows, got.shape[0])
-        plan = Plan(first_group, groups, first, last, beyond, send, spot)
+        plan = Plan(first_group, groups, first, last, beyond, send, not end, spot)
         fulls, sent, weights, carry, gacc = chunk_call(
             plan, norm, counts, nodes_in, cotangent, halo, weights, carry, gacc, fulls, got
         )
         if send:
             waiting.append((row, lax.ppermute(sent, "head", swap)))
+        if last:
+            grads = gacc.reshape(heads * places, 1024 // places, 128)
+            grads = lax.all_to_all(grads, ("head", "gz", "tile"), 0, 0, tiled=True)
+        if n == own_count:
+            grads, *fulls = lax.optimization_barrier((grads, *fulls))
         first_group += groups
         row += plan.rows
 
-    part = 1024 // places
-    grads = gacc.reshape(heads * places, part, 128)
-    grads = lax.all_to_all(grads, ("head", "gz", "tile"), 0, 0, tiled=True)
     share = jnp.sum(grads.astype(F32), axis=0).astype(BF)
-    share, *fulls = lax.optimization_barrier((share, *fulls))
     share = jnp.broadcast_to(share[None], (places,) + share.shape)
     whole = lax.all_to_all(share, ("gz", "tile"), 0, 0, tiled=True).reshape(1024, 128).astype(F32)
-    grad_out = jnp.concatenate([whole[768:896], whole[896:1024]], 1)
+    grad_out = whole[768:1024].reshape(16, 2, 8, 128).transpose(0, 2, 1, 3).reshape(128, 256)
     return (fulls[0], fulls[1], whole[0:256], whole[256:512], whole[512:768], grad_out)
 
 

time: 104 us -> 99.2 us (0.954)
  blocking collectives: 18.5 us -> 0 us
  starting transfers between devices: 18.2 us -> 25.9 us
  Pallas kernels: 54.1 us -> 58.2 us
  waiting for transfers between devices: 6.94 us -> 8.5 us
    all_to_all x1 -> x0, blocking collectives: 18.5 us -> none  [per_device(): lax.all_to_all(share, ('gz', 'tile'), 0, 0, tiled=True).reshape(1024, 128)]
    all_to_all x0 -> x1, starting transfers between devices: none -> 8.77 us  [per_device(): lax.all_to_all(share, ('gz', 'tile'), 0, 0, tiled=True).reshape(1024, 128)]
    pallas_call x4, Pallas kernels: 51.3 us -> 56.3 us  [chunk_call(): pl.pallas_call(functools.partial(chunk_kernel, plan, norm), out_shape=out...]
    ppermute x2 -> x1, starting transfers between devices: 3.31 us -> 1.06 us  [per_device(): waiting.append((row, lax.ppermute(sent, 'head', swap)))]
    all_to_all x0 -> x1, waiting for transfers between devices: none -> 1.56 us  [per_device(): lax.all_to_all(share, ('gz', 'tile'), 0, 0, tiled=True).reshape(1024, 128)]
    all_to_all x1, starting transfers between devices: 10.5 us -> 11.7 us  [per_device(): grads = lax.all_to_all(grads, ('head', 'gz', 'tile'), 0, 0, tiled=True)]
    unnamed x8 -> x6, local copies, waits for them, and re-layouts: 2.63 us -> 1.77 us
  transfers between devices with their start and end apart: 5 -> 5, of which waited for: 2 -> 3; matrix products, arithmetic and copies ran while one was open for 0% -> 0% of each run, Pallas kernels for 37% -> 41%
where the time goes in v3:
time: 99.2 us; the launch traced here: 97.4 us
  Pallas kernels  58.2 us (59%)
  starting transfers between devices  25.9 us (26%)
  waiting for transfers between devices  8.5 us (9%)
  local copies, waits for them, and re-layouts  3.92 us (4%)
    pallas_call x4, Pallas kernels, chunk_call(): pl.pallas_call(functools.partial(chunk_kernel, plan, norm), out_shape=out...  56.3 us
    all_to_all x1, starting transfers between devices, per_device(): grads = lax.all_to_all(grads, ('head', 'gz', 'tile'), 0, 0, tiled=True)  11.7 us
    all_to_all x1, starting transfers between devices, per_device(): lax.all_to_all(share, ('gz', 'tile'), 0, 0, tiled=True).reshape(1024, 128)  8.77 us
    ppermute x1, waiting for transfers between devices, per_device(): halo = lax.ppermute(rims, ('gz', 'head', 'tile'), route)  6.44 us
    ppermute x1, starting transfers between devices, per_device(): halo = lax.ppermute(rims, ('gz', 'head', 'tile'), route)  4.4 us
  transfers between devices with their start and end apart: 5, of which 3 were waited for; matrix products, arithmetic and copies ran while one was open for 0% of the time, Pallas kernels for 41%

profile of v3, /device:TPU:17, one launch (start us, length us, event | category | flops | bytes accessed | tf_op | source)
XLA Modules:
  0.0 97.4 jit_solution(2790939151910518812)
XLA Ops:
  0.6 1.9 %shard_map.118 = (bf16[1024,128]{1,0:T(8,128)(2,1)}, bf16[256,512]{1,0:T(8,128)(2,1)}) custom-call(bf16[8192,256]{1,0:T(8,128)(2,1)} %refs_1_.7, bf16[8192,256]{1,0:T(8,128)(2,1)} %refs_2_.7, bf16[256,128]{1,0:T(8,128)(2,1)} %wq.1, bf16[256,128]{1,0:T(8,128)(2,1)} %wk.1, bf16[256,128]{1,0:T(8,128)(2,1)} %wv.1, bf16[128,256]{1,0:T(8,128)(2,1)} %wo.1), custom_call_target="tpu_custom_call" | custom-call | tf_op jit(solution)/shard_map/pallas_call | solution.py:488
  2.6 4.4 %collective-permute-start = (bf16[256,512]{1,0:T(8,128)(2,1)}, bf16[256,512]{1,0:T(8,128)(2,1)S(1)}, u32[]{:S(2)}, u32[]{:S(2)}) collective-permute-start(bf16[256,512]{1,0:T(8,128)(2,1)} %get-tuple-element.35), channel_id=1, source_target_pairs={{0,1},{1,2},{2,3},{3,8},{8,9},{9,10},{10,11},{11,16},{16,17},{17,1... | collective-permute-start | bytes 786440 | tf_op jit(solution)/shard_map/ppermute | solution.py:510
  7.0 0.0 collective-permute-start.1
  7.0 6.4 %collective-permute-done.refs_3_ = bf16[256,512]{1,0:T(8,128)(2,1)S(1)} collective-permute-done((bf16[256,512]{1,0:T(8,128)(2,1)}, bf16[256,512]{1,0:T(8,128)(2,1)S(1)}, u32[]{:S(2)}, u32[]{:S(2)}) %collective-permute-start) | collective-permute-done | bytes 262176 | tf_op jit(solution)/shard_map/ppermute | solution.py:510
  13.4 0.0 copy-start.1
  13.4 0.5 collective-permute-done.1.refs_5_
  13.9 0.2 copy-done.1
  14.1 0.0 copy-start.2
  14.1 0.7 copy-done.2
  14.8 16.4 %shard_map.119 = (bf16[8192,128]{1,0:T(8,128)(2,1)}, bf16[8192,128]{1,0:T(8,128)(2,1)}, bf16[1536,256]{1,0:T(8,128)(2,1)}, bf16[256,768]{1,0:T(8,128)(2,1)}, bf1...) custom-call(s32[4096]{0:T(1024)} %refs_0_.7, ...), custom_call_target="tpu_custom_call" | custom-call | flops 6144000000 | bytes 1536000 | tf_op jit(solution)/shard_map/pallas_call | solution.py:444
  31.2 1.1 %collective-permute-start.2 = (bf16[1536,256]{1,0:T(8,128)(2,1)}, bf16[1536,256]{1,0:T(8,128)(2,1)S(1)}, u32[]{:S(2)}, u32[]{:S(2)}) collective-permute-start(bf16[1536,256]{1,0:T(8,128)(2,1)} %get-tuple-element.52), channel_id=1, source_target_pairs={{0,4},{4,0},{1,5},{5,1},{2,6},{6,2},{3,7},{7,3},{8,12},{12,8},{9,1... | collective-permute-start | bytes 2359304 | tf_op jit(solution)/shard_map/ppermute | solution.py:528
  32.3 19.7 %shard_map.120 = (bf16[8192,128]{1,0:T(8,128)(2,1)}, bf16[8192,128]{1,0:T(8,128)(2,1)}, bf16[256,512]{1,0:T(8,128)(2,1)}, bf16[256,512]{1,0:T(8,128)(2,1)}, bf16...) custom-call(s32[4096]{0:T(1024)} %refs_0_.7, ...), custom_call_target="tpu_custom_call", output_to_operand_aliasing={{0}: (11, {}), {1}: (12, {})} | custom-call | flops 10240000000 | bytes 2560000 | tf_op jit(solution)/shard_map/pallas_call | solution.py:444
  52.0 11.7 %all-to-all-start = ((bf16[128,16,128]{2,1,0:T(8,128)(2,1)}), bf16[128,16,128]{2,1,0:T(8,128)(2,1)S(1)}, u32[]{:S(2)}, u32[]{:S(2)}) async-start(bf16[128,16,128]{2,1,0:T(8,128)(2,1)} %bitcast.10), calls=%async_computation | async-start | bytes 1048576 | tf_op jit(solution)/shard_map/all_to_all | solution.py:531
  63.6 0.0 collective-permute-done.2.refs_12_
  63.6 0.0 copy-start
  63.7 0.9 copy-done
  64.5 11.9 %shard_map.121 = (bf16[8192,128]{1,0:T(8,128)(2,1)}, bf16[8192,128]{1,0:T(8,128)(2,1)}, bf16[256,512]{1,0:T(8,128)(2,1)}, bf16[256,512]{1,0:T(8,128)(2,1)}, bf16[256,512]{1,0:T(8,128)(2,1)}) custom-call(s32[4096]{0:T(1024)} %refs_0_.7, bf16[8192,256]{1,0:T(8,128)(2,1)} %refs_1_.7, ...), custom_call_target="tpu_custom_call", output_to_operand_aliasing={{0}: (10, {}), {1}: (11, {})} | custom-call | flops 307200000 | bytes 1536000 | tf_op jit(solution)/shard_map/pallas_call | solution.py:444
  76.4 0.0 all-to-all-done
  76.4 0.1 reduce_sum.12
  76.6 0.7 broadcast_in_dim.2
  77.3 8.8 %all-to-all-start.1 = ((bf16[64,16,128]{2,1,0:T(8,128)(2,1)}), bf16[64,16,128]{2,1,0:T(8,128)(2,1)S(1)}, u32[]{:S(2)}, u32[]{:S(2)}) async-start(bf16[64,16,128]{2,1,0:T(8,128)(2,1)} %broadcast_in_dim.2), calls=%async_computation.1 | async-start | bytes 524288 | tf_op jit(solution)/shard_map/all_to_all | solution.py:539
  86.1 8.3 %shard_map.122 = (bf16[8192,128]{1,0:T(8,128)(2,1)}, bf16[8192,128]{1,0:T(8,128)(2,1)}) custom-call(s32[4096]{0:T(1024)} %refs_0_.7, bf16[8192,256]{1,0:T(8,128)(2,1)} %refs_1_.7, bf16[8192,256]{1,0:T(8,128)(2,1)} %refs_2_.7, bf16[256,768]{1,0:T(8,128)(2,1)} %get-tuple-element.37.refs_3_, ...), custom_call_target="tpu_custom_call", output_to_operand_aliasing={{0}: (10, {}), {1}: (11, {})} | custom-call | flops 204800000 | bytes 1024000 | tf_op jit(solution)/shard_map/pallas_call | solution.py:444
  94.4 1.6 %all-to-all-done.1 = bf16[64,16,128]{2,1,0:T(8,128)(2,1)S(1)} async-done(((bf16[64,16,128]{2,1,0:T(8,128)(2,1)}), bf16[64,16,128]{2,1,0:T(8,128)(2,1)S(1)}, u32[]{:S(2)}, u32[]{:S(2)}) %all-to-all-start.1) | async-done | bytes 262176 | tf_op jit(solution)/shard_map/all_to_all | solution.py:539
  96.0 0.7 slice_bitcast_fusion
  96.7 0.8 fusion
  (1 shorter events, 0.0 us)
Async XLA Ops:
  2.6 10.8 %collective-permute-start = (bf16[256,512]{1,0:T(8,128)(2,1)}, bf16[256,512]{1,0:T(8,128)(2,1)S(1)}, u32[]{:S(2)}, u32[]{:S(2)}) collective-permute-start(bf16[256,512]{1,0:T(8,128)(2,1)} %get-tuple-element.35), channel_id=1, source_target_pairs={{0,1},{1,2},{2,3},{3,8},{8,9},{9,10},{10,11},{11,16},{16,17},{17,1... | collective-permute-start | bytes 786440 | tf_op jit(solution)/shard_map/ppermute | solution.py:510
  7.0 6.9 %collective-permute-start.1 = (bf16[1024,128]{1,0:T(8,128)(2,1)}, bf16[1024,128]{1,0:T(8,128)(2,1)S(1)}, u32[]{:S(2)}, u32[]{:S(2)}) collective-permute-start(bf16[1024,128]{1,0:T(8,128)(2,1)} %get-tuple-element.36.refs_4_), channel_id=1, source_target_pairs={{0,4},{4,0},{1,5},{5,1},{2,6},{6,2},{3,7},{7,3},{8,12},{12,8},{9,1... | collective-permute-start | bytes 786440 | tf_op jit(solution)/shard_map/ppermute | solution.py:507
  13.4 0.7 copy-start.1
  14.1 0.7 copy-start.2
  31.2 32.4 %collective-permute-start.2 = (bf16[1536,256]{1,0:T(8,128)(2,1)}, bf16[1536,256]{1,0:T(8,128)(2,1)S(1)}, u32[]{:S(2)}, u32[]{:S(2)}) collective-permute-start(bf16[1536,256]{1,0:T(8,128)(2,1)} %get-tuple-element.52), channel_id=1, source_target_pairs={{0,4},{4,0},{1,5},{5,1},{2,6},{6,2},{3,7},{7,3},{8,12},{12,8},{9,1... | collective-permute-start | bytes 2359304 | tf_op jit(solution)/shard_map/ppermute | solution.py:528
  52.0 24.5 %all-to-all-start = ((bf16[128,16,128]{2,1,0:T(8,128)(2,1)}), bf16[128,16,128]{2,1,0:T(8,128)(2,1)S(1)}, u32[]{:S(2)}, u32[]{:S(2)}) async-start(bf16[128,16,128]{2,1,0:T(8,128)(2,1)} %bitcast.10), calls=%async_computation | async-start | bytes 1048576 | tf_op jit(solution)/shard_map/all_to_all | solution.py:531
  63.6 0.9 copy-start
  77.3 18.7 %all-to-all-start.1 = ((bf16[64,16,128]{2,1,0:T(8,128)(2,1)}), bf16[64,16,128]{2,1,0:T(8,128)(2,1)S(1)}, u32[]{:S(2)}, u32[]{:S(2)}) async-start(bf16[64,16,128]{2,1,0:T(8,128)(2,1)} %broadcast_in_dim.2), calls=%async_computation.1 | async-start | bytes 524288 | tf_op jit(solution)/shard_map/all_to_all | solution.py:539

commit v4 on v3

--- a/solution.py
+++ b/solution.py
@@ -212,25 +212,27 @@
     def ready_of(base, part):
         return base - HALO + part * HALO + side * (3 * HALO - 2 * HALO * part)
 
-    def result_copies(i):
-        start = pl.multiple_of(ready_of(base_of(i), 0) - side * HALO, HALO)
-        here = pl.ds(start, GROUP)
-        final = pl.ds(pl.multiple_of(origin + start, HALO), GROUP)
+    def half_copies(i, part):
+        start = pl.multiple_of(ready_of(base_of(i), part), HALO)
+        here = pl.ds(start, HALO)
+        final = pl.ds(pl.multiple_of(origin + start, HALO), HALO)
         found = [
-            pltpu.make_async_copy(keep_o.at[here], out_full.at[final], out_sems.at[i, 0]),
-            pltpu.make_async_copy(keep_g.at[here], gn_full.at[final], out_sems.at[i, 1]),
+            pltpu.make_async_copy(keep_o.at[here], out_full.at[final], out_sems.at[i, 3 * part]),
+            pltpu.make_async_copy(keep_g.at[here], gn_full.at[final], out_sems.at[i, 3 * part + 1]),
         ]
         if plan.send:
             first_row = (1 - side) * (GROUP if first else 0) + side * HALO
-            there = pl.ds(pl.multiple_of(start - first_row, HALO), GROUP)
-            found.append(pltpu.make_async_copy(send_st.at[here], send.at[there], out_sems.at[i, 2]))
+            there = pl.ds(pl.multiple_of(start - first_row, HALO), HALO)
+            found.append(pltpu.make_async_copy(send_st.at[here], send.at[there], out_sems.at[i, 3 * part + 2]))
         return found
 
-    def step(i, with_finish):
+    def wait_group(i):
+        wait_piece(2 * i + 1)
+        wait_piece(2 * i + 2)
+
+    def project(i, slot):
         base = pl.multiple_of(base_of(i), HALO)
         here = pl.ds(base, GROUP)
-        wait_piece(2 * i + 1)
-        wait_piece(2 * i + 2)
         for b in range(4):
             mask_cot(base + b * WINDOW)
         proj = mm(xs[here, :], wqkv[...])
@@ -238,13 +240,57 @@
         near_in[here, 0:384] = proj[:, 0:384].astype(BF)
         near_in[here, 384:512] = dctx[:, 0:128].astype(BF)
         for j in range(3):
-            far_stage[j] = proj[:, 384 + 128 * j : 512 + 128 * j]
-        far_stage[3] = dctx[:, 128:256]
+            far_stage[slot, j] = proj[:, 384 + 128 * j : 512 + 128 * j]
+        far_stage[slot, 3] = dctx[:, 128:256]
+
+    def turn(i, part):
+        half = pl.ds(pl.multiple_of(ready_of(base_of(i), part), HALO), HALO)
+        return (xs[half, :].T, cs[half, :].T) if grads_on else None
+
+    def finish(i, part, turned):
+        start = pl.multiple_of(ready_of(base_of(i), part), HALO)
+        ready = pl.ds(start, HALO)
+        near = near_out[ready, :]
+        far = far_out[ready, :]
+        ctx = jnp.concatenate([near[:, :128], far[:, :128]], 1)
+        grads = jnp.concatenate([near[:, 128:], far[:, 128:]], 1)
+        wp, wt = (wout_p, wqkv_t) if plan.send else (wout_p.at[:, pl.ds(0, 128)], wqkv_t.at[:, pl.ds(0, 128)])
+        out = mm(ctx, wp[...])
+        parts = []
+        for q in range(2):
+            rows = slice(q * WINDOW, (q + 1) * WINDOW)
+            keep = wide_iota[:, : out.shape[1]] < count_of(start + q * WINDOW)
+            parts.append(jnp.where(keep, out[rows], 0.0))
+        out = jnp.concatenate(parts, 0).astype(BF)
+        gn = mm(grads, wt[...]).astype(BF)
+        keep_o[ready, :] = out[:, :128]
+        keep_g[ready, :] = gn[:, :128]
+        if plan.send:
+            send_st[ready, 0:128] = out[:, 128:]
+            send_st[ready, 128:256] = gn[:, 128:]
+        if grads_on:
+            gacc[:, 0:768] += mm(turned[0], grads)
+            gacc[:, 768:1024] += mm(turned[1], ctx)
+
+    def step(i, before, with_finish):
+        base = pl.multiple_of(base_of(i), HALO)
+        here = pl.ds(base, GROUP)
+        following = jnp.minimum(i + 1, groups - 1)
+        slot = lax.rem(i, 2)
+        if isinstance(i, int):
+            if i + 1 < groups:
+                wait_group(i + 1)
+        else:
+
+            @pl.when(i + 1 < groups)
+            def _():
+                wait_group(i + 1)
+
         spread = head_masks()
 
         def far_window(r):
             def load():
-                return [far_stage[j, pl.ds(r, WINDOW, stride=4), :].astype(BF) for j in range(4)]
+                return [far_stage[slot, j, pl.ds(r, WINDOW, stride=4), :].astype(BF) for j in range(4)]
 
             def mask():
                 quarter = row_iota // 32
@@ -279,35 +325,10 @@
 
             return Window(load, mask, store, spread)
 
-        def finish(part):
-            start = pl.multiple_of(ready_of(base, part), HALO)
-            ready = pl.ds(start, HALO)
-            near = near_out[ready, :]
-            far = far_out[ready, :]
-            ctx = jnp.concatenate([near[:, :128], far[:, :128]], 1)
-            grads = jnp.concatenate([near[:, 128:], far[:, 128:]], 1)
-            wp, wt = (wout_p, wqkv_t) if plan.send else (wout_p.at[:, pl.ds(0, 128)], wqkv_t.at[:, pl.ds(0, 128)])
-            out = mm(ctx, wp[...])
-            parts = []
-            for q in range(2):
-                rows = slice(q * WINDOW, (q + 1) * WINDOW)
-                keep = wide_iota[:, : out.shape[1]] < count_of(start + q * WINDOW)
-                parts.append(jnp.where(keep, out[rows], 0.0))
-            out = jnp.concatenate(parts, 0).astype(BF)
-            gn = mm(grads, wt[...]).astype(BF)
-            keep_o[ready, :] = out[:, :128]
-            keep_g[ready, :] = gn[:, :128]
-            if plan.send:
-                send_st[ready, 0:128] = out[:, 128:]
-                send_st[ready, 128:256] = gn[:, 128:]
-            if grads_on:
-                gacc[:, 0:768] += mm(turned_x[part], grads)
-                gacc[:, 768:1024] += mm(turned_c[part], ctx)
-
-        if with_finish and grads_on:
-            halves = [pl.ds(pl.multiple_of(ready_of(base, p), HALO), HALO) for p in range(2)]
-            turned_x = [xs[half, :].T for half in halves]
-            turned_c = [cs[half, :].T for half in halves]
+        if before:
+            turned_before = turn(i - 1, 1)
+        if with_finish:
+            turned = turn(i, 0)
 
         line = [near_window(0)] + [far_window(r) for r in range(4)] + [near_window(k) for k in range(1, 4)]
         count = len(line)
@@ -318,20 +339,27 @@
                 line[t - 1].softmax()
             if t >= 2:
                 line[t - 2].outputs()
+            if t == 1 and before:
+                finish(i - 1, 1, turned_before)
             if t == 3 and with_finish:
-                finish(0)
+                finish(i, 0, turned)
             if t == 6:
                 for j in range(4):
                     far_out[here, 128 * j : 128 * j + 128] = far_res[j].astype(BF)
-        if with_finish:
-            finish(1)
-            for copy in result_copies(i):
+            if t == 8:
+                project(following, 1 - slot)
+        halves = ([(i - 1, 1)] if before else []) + ([(i, 0)] if with_finish else [])
+        for group, part in halves:
+            for copy in half_copies(group, part):
                 copy.start()
 
-    start = 0
-    if first:
-        step(0, False)
-        start = 1
+    wait_group(0)
+    project(0, 0)
+    start = 1
+    step(0, False, not first)
+    if first:
+        step(1, False, True)
+        start = 2
     if plan.got:
         got_load.wait()
         row, size = plan.got
@@ -345,10 +373,13 @@
             copy.start()
 
     def loop_body(i, _):
-        step(i, True)
+        step(i, True, True)
         return 0
 
     lax.fori_loop(start, groups, loop_body, 0)
+    finish(groups - 1, 1, turn(groups - 1, 1))
+    for copy in half_copies(groups - 1, 1):
+        copy.start()
 
     passed = []
     if plan.carry:
@@ -377,8 +408,9 @@
     for copy in passed:
         copy.wait()
     for i in range(1 if first else 0, groups):
-        for copy in result_copies(i):
-            copy.wait()
+        for part in range(2):
+            for copy in half_copies(i, part):
+                copy.wait()
     if plan.got:
         for copy in got_copies:
             copy.wait()
@@ -423,7 +455,7 @@
         pltpu.VMEM((buffer, 512), BF),
         pltpu.VMEM((buffer, 512), BF),
         pltpu.VMEM((buffer, 512), BF),
-        pltpu.VMEM((4, GROUP, 128), F32),
+        pltpu.VMEM((2, 4, GROUP, 128), F32),
         pltpu.VMEM((4, GROUP, 128), F32),
         pltpu.VMEM((256, 1024), F32),
         pltpu.VMEM((256, 1024), F32),
@@ -433,7 +465,7 @@
         pltpu.SMEM((counts.shape[0],), jnp.int32),
         pltpu.SemaphoreType.DMA((2 * groups + 1, 2)),
         pltpu.SemaphoreType.DMA((9,)),
-        pltpu.SemaphoreType.DMA((groups, 3)),
+        pltpu.SemaphoreType.DMA((groups, 6)),
     ]
     if first:
         scratch += [pltpu.VMEM((1024, 128), BF)] * 2

time: 99.2 us -> 96.7 us (0.975)
  Pallas kernels: 58.2 us -> 55.5 us
    pallas_call x4, Pallas kernels: 56.3 us -> 53.6 us  [chunk_call(): pl.pallas_call(functools.partial(chunk_kernel, plan, norm), out_shape=out...]
  transfers between devices with their start and end apart: 5 -> 5, of which waited for: 3 -> 3; matrix products, arithmetic and copies ran while one was open for 0% -> 0% of each run, Pallas kernels for 41% -> 40%
where the time goes in v4:
time: 96.7 us; the launch traced here: 95 us
  Pallas kernels  55.5 us (57%)
  starting transfers between devices  26.1 us (27%)
  waiting for transfers between devices  8.56 us (9%)
  local copies, waits for them, and re-layouts  3.92 us (4%)
    pallas_call x4, Pallas kernels, chunk_call(): pl.pallas_call(functools.partial(chunk_kernel, plan, norm), out_shape=out...  53.6 us
    all_to_all x1, starting transfers between devices, per_device(): grads = lax.all_to_all(grads, ('head', 'gz', 'tile'), 0, 0, tiled=True)  11.7 us
    all_to_all x1, starting transfers between devices, per_device(): lax.all_to_all(share, ('gz', 'tile'), 0, 0, tiled=True).reshape(1024, 128)  8.77 us
    ppermute x1, waiting for transfers between devices, per_device(): halo = lax.ppermute(rims, ('gz', 'head', 'tile'), route)  6.44 us
    ppermute x1, starting transfers between devices, per_device(): halo = lax.ppermute(rims, ('gz', 'head', 'tile'), route)  4.4 us
    pallas_call x1, Pallas kernels, pack_call(): pl.pallas_call(pack_kernel, out_shape=(jax.ShapeDtypeStruct((1024, 128),...  1.94 us
  transfers between devices with their start and end apart: 5, of which 3 were waited for; matrix products, arithmetic and copies ran while one was open for 0% of the time, Pallas kernels for 40%

profile of v4, /device:TPU:17, one launch (start us, length us, event | category | flops | bytes accessed | tf_op | source)
XLA Modules:
  0.0 95.0 jit_solution(2967061891750887725)
XLA Ops:
  0.6 1.9 %shard_map.118 = (bf16[1024,128]{1,0:T(8,128)(2,1)}, bf16[256,512]{1,0:T(8,128)(2,1)}) custom-call(bf16[8192,256]{1,0:T(8,128)(2,1)} %refs_1_.7, bf16[8192,256]{1,0:T(8,128)(2,1)} %refs_2_.7, bf16[256,128]{1,0:T(8,128)(2,1)} %wq.1, bf16[256,128]{1,0:T(8,128)(2,1)} %wk.1, bf16[256,128]{1,0:T(8,128)(2,1)} %wv.1, bf16[128,256]{1,0:T(8,128)(2,1)} %wo.1), custom_call_target="tpu_custom_call" | custom-call | tf_op jit(solution)/shard_map/pallas_call | solution.py:520
  2.6 4.4 %collective-permute-start = (bf16[256,512]{1,0:T(8,128)(2,1)}, bf16[256,512]{1,0:T(8,128)(2,1)S(1)}, u32[]{:S(2)}, u32[]{:S(2)}) collective-permute-start(bf16[256,512]{1,0:T(8,128)(2,1)} %get-tuple-element.35), channel_id=1, source_target_pairs={{0,1},{1,2},{2,3},{3,8},{8,9},{9,10},{10,11},{11,16},{16,17},{17,1... | collective-permute-start | bytes 786440 | tf_op jit(solution)/shard_map/ppermute | solution.py:542
  7.0 0.0 collective-permute-start.1
  7.0 6.4 %collective-permute-done.refs_3_ = bf16[256,512]{1,0:T(8,128)(2,1)S(1)} collective-permute-done((bf16[256,512]{1,0:T(8,128)(2,1)}, bf16[256,512]{1,0:T(8,128)(2,1)S(1)}, u32[]{:S(2)}, u32[]{:S(2)}) %collective-permute-start) | collective-permute-done | bytes 262176 | tf_op jit(solution)/shard_map/ppermute | solution.py:542
  13.4 0.0 copy-start.1
  13.4 0.5 collective-permute-done.1.refs_5_
  13.9 0.2 copy-done.1
  14.1 0.0 copy-start.2
  14.1 0.7 copy-done.2
  14.8 15.6 %shard_map.119 = (bf16[8192,128]{1,0:T(8,128)(2,1)}, bf16[8192,128]{1,0:T(8,128)(2,1)}, bf16[1536,256]{1,0:T(8,128)(2,1)}, bf16[256,768]{1,0:T(8,128)(2,1)}, bf1...) custom-call(s32[4096]{0:T(1024)} %refs_0_.7, ...), custom_call_target="tpu_custom_call" | custom-call | flops 6144000000 | bytes 1536000 | tf_op jit(solution)/shard_map/pallas_call | solution.py:476
  30.4 1.3 %collective-permute-start.2 = (bf16[1536,256]{1,0:T(8,128)(2,1)}, bf16[1536,256]{1,0:T(8,128)(2,1)S(1)}, u32[]{:S(2)}, u32[]{:S(2)}) collective-permute-start(bf16[1536,256]{1,0:T(8,128)(2,1)} %get-tuple-element.52), channel_id=1, source_target_pairs={{0,4},{4,0},{1,5},{5,1},{2,6},{6,2},{3,7},{7,3},{8,12},{12,8},{9,1... | collective-permute-start | bytes 2359304 | tf_op jit(solution)/shard_map/ppermute | solution.py:560
  31.7 18.5 %shard_map.120 = (bf16[8192,128]{1,0:T(8,128)(2,1)}, bf16[8192,128]{1,0:T(8,128)(2,1)}, bf16[256,512]{1,0:T(8,128)(2,1)}, bf16[256,512]{1,0:T(8,128)(2,1)}, bf16...) custom-call(s32[4096]{0:T(1024)} %refs_0_.7, ...), custom_call_target="tpu_custom_call", output_to_operand_aliasing={{0}: (11, {}), {1}: (12, {})} | custom-call | flops 10240000000 | bytes 2560000 | tf_op jit(solution)/shard_map/pallas_call | solution.py:476
  50.3 11.7 %all-to-all-start = ((bf16[128,16,128]{2,1,0:T(8,128)(2,1)}), bf16[128,16,128]{2,1,0:T(8,128)(2,1)S(1)}, u32[]{:S(2)}, u32[]{:S(2)}) async-start(bf16[128,16,128]{2,1,0:T(8,128)(2,1)} %bitcast.10), calls=%async_computation | async-start | bytes 1048576 | tf_op jit(solution)/shard_map/all_to_all | solution.py:563
  61.9 0.0 collective-permute-done.2.refs_12_
  61.9 0.0 copy-start
  61.9 0.9 copy-done
  62.8 11.1 %shard_map.121 = (bf16[8192,128]{1,0:T(8,128)(2,1)}, bf16[8192,128]{1,0:T(8,128)(2,1)}, bf16[256,512]{1,0:T(8,128)(2,1)}, bf16[256,512]{1,0:T(8,128)(2,1)}, bf16[256,512]{1,0:T(8,128)(2,1)}) custom-call(s32[4096]{0:T(1024)} %refs_0_.7, bf16[8192,256]{1,0:T(8,128)(2,1)} %refs_1_.7, ...), custom_call_target="tpu_custom_call", output_to_operand_aliasing={{0}: (10, {}), {1}: (11, {})} | custom-call | flops 307200000 | bytes 1536000 | tf_op jit(solution)/shard_map/pallas_call | solution.py:476
  74.0 0.0 all-to-all-done
  74.0 0.1 reduce_sum.12
  74.1 0.7 broadcast_in_dim.2
  74.9 8.8 %all-to-all-start.1 = ((bf16[64,16,128]{2,1,0:T(8,128)(2,1)}), bf16[64,16,128]{2,1,0:T(8,128)(2,1)S(1)}, u32[]{:S(2)}, u32[]{:S(2)}) async-start(bf16[64,16,128]{2,1,0:T(8,128)(2,1)} %broadcast_in_dim.2), calls=%async_computation.1 | async-start | bytes 524288 | tf_op jit(solution)/shard_map/all_to_all | solution.py:571
  83.6 8.2 %shard_map.122 = (bf16[8192,128]{1,0:T(8,128)(2,1)}, bf16[8192,128]{1,0:T(8,128)(2,1)}) custom-call(s32[4096]{0:T(1024)} %refs_0_.7, bf16[8192,256]{1,0:T(8,128)(2,1)} %refs_1_.7, bf16[8192,256]{1,0:T(8,128)(2,1)} %refs_2_.7, bf16[256,768]{1,0:T(8,128)(2,1)} %get-tuple-element.37.refs_3_, ...), custom_call_target="tpu_custom_call", output_to_operand_aliasing={{0}: (10, {}), {1}: (11, {})} | custom-call | flops 204800000 | bytes 1024000 | tf_op jit(solution)/shard_map/pallas_call | solution.py:476
  91.9 1.6 %all-to-all-done.1 = bf16[64,16,128]{2,1,0:T(8,128)(2,1)S(1)} async-done(((bf16[64,16,128]{2,1,0:T(8,128)(2,1)}), bf16[64,16,128]{2,1,0:T(8,128)(2,1)S(1)}, u32[]{:S(2)}, u32[]{:S(2)}) %all-to-all-start.1) | async-done | bytes 262176 | tf_op jit(solution)/shard_map/all_to_all | solution.py:571
  93.6 0.7 slice_bitcast_fusion
  94.2 0.8 fusion
  (1 shorter events, 0.0 us)
Async XLA Ops:
  2.6 10.8 %collective-permute-start = (bf16[256,512]{1,0:T(8,128)(2,1)}, bf16[256,512]{1,0:T(8,128)(2,1)S(1)}, u32[]{:S(2)}, u32[]{:S(2)}) collective-permute-start(bf16[256,512]{1,0:T(8,128)(2,1)} %get-tuple-element.35), channel_id=1, source_target_pairs={{0,1},{1,2},{2,3},{3,8},{8,9},{9,10},{10,11},{11,16},{16,17},{17,1... | collective-permute-start | bytes 786440 | tf_op jit(solution)/shard_map/ppermute | solution.py:542
  7.0 6.9 %collective-permute-start.1 = (bf16[1024,128]{1,0:T(8,128)(2,1)}, bf16[1024,128]{1,0:T(8,128)(2,1)S(1)}, u32[]{:S(2)}, u32[]{:S(2)}) collective-permute-start(bf16[1024,128]{1,0:T(8,128)(2,1)} %get-tuple-element.36.refs_4_), channel_id=1, source_target_pairs={{0,4},{4,0},{1,5},{5,1},{2,6},{6,2},{3,7},{7,3},{8,12},{12,8},{9,1... | collective-permute-start | bytes 786440 | tf_op jit(solution)/shard_map/ppermute | solution.py:539
  13.4 0.7 copy-start.1
  14.1 0.7 copy-start.2
  30.4 31.5 %collective-permute-start.2 = (bf16[1536,256]{1,0:T(8,128)(2,1)}, bf16[1536,256]{1,0:T(8,128)(2,1)S(1)}, u32[]{:S(2)}, u32[]{:S(2)}) collective-permute-start(bf16[1536,256]{1,0:T(8,128)(2,1)} %get-tuple-element.52), channel_id=1, source_target_pairs={{0,4},{4,0},{1,5},{5,1},{2,6},{6,2},{3,7},{7,3},{8,12},{12,8},{9,1... | collective-permute-start | bytes 2359304 | tf_op jit(solution)/shard_map/ppermute | solution.py:560
  50.3 23.7 %all-to-all-start = ((bf16[128,16,128]{2,1,0:T(8,128)(2,1)}), bf16[128,16,128]{2,1,0:T(8,128)(2,1)S(1)}, u32[]{:S(2)}, u32[]{:S(2)}) async-start(bf16[128,16,128]{2,1,0:T(8,128)(2,1)} %bitcast.10), calls=%async_computation | async-start | bytes 1048576 | tf_op jit(solution)/shard_map/all_to_all | solution.py:563
  61.9 0.9 copy-start
  74.9 18.7 %all-to-all-start.1 = ((bf16[64,16,128]{2,1,0:T(8,128)(2,1)}), bf16[64,16,128]{2,1,0:T(8,128)(2,1)S(1)}, u32[]{:S(2)}, u32[]{:S(2)}) async-start(bf16[64,16,128]{2,1,0:T(8,128)(2,1)} %broadcast_in_dim.2), calls=%async_computation.1 | async-start | bytes 524288 | tf_op jit(solution)/shard_map/all_to_all | solution.py:571

commit v5 on v4

--- a/solution.py
+++ b/solution.py
@@ -156,18 +156,19 @@
         piece = k + side * (2 * groups - 2 * k)
         return piece, pl.ds(pl.multiple_of(piece * HALO, HALO), HALO)
 
-    copies = [pltpu.make_async_copy(counts_hbm, counts, misc_sems.at[0])]
+    copies, late = [pltpu.make_async_copy(counts_hbm, counts, misc_sems.at[0])], []
     if first:
         copies.append(pltpu.make_async_copy(own_hbm, own_ref, misc_sems.at[1]))
         copies.append(pltpu.make_async_copy(oth_hbm, oth_ref, misc_sems.at[2]))
     else:
         for k in range(4):
-            copies.append(pltpu.make_async_copy(weights_c[k], weights[k], misc_sems.at[1 + k]))
+            use = copies if k in (0, 2) else late
+            use.append(pltpu.make_async_copy(weights_c[k], weights[k], misc_sems.at[1 + k]))
         for k, buffer in enumerate((near_in, near_out, far_out)):
-            copies.append(pltpu.make_async_copy(carry_c[k], buffer.at[carry_in], misc_sems.at[5 + k]))
+            late.append(pltpu.make_async_copy(carry_c[k], buffer.at[carry_in], misc_sems.at[5 + k]))
     for copy in copies:
         copy.start()
-    for k in range(1 if first else 0, 2 * groups + 1):
+    for k in list(range(1, 2 * groups + 1)) + ([] if first else [0]):
         piece, dst = piece_place(k)
         if first and k == 1:
             pltpu.make_async_copy(halo_hbm.at[:, pl.ds(0, 256)], xs.at[dst], in_sems.at[k, 0]).start()
@@ -176,6 +177,8 @@
             src = pl.ds(pl.multiple_of(origin + piece * HALO, HALO), HALO)
             pltpu.make_async_copy(x_hbm.at[src], xs.at[dst], in_sems.at[k, 0]).start()
             pltpu.make_async_copy(c_hbm.at[src], cs.at[dst], in_sems.at[k, 1]).start()
+    for copy in late:
+        copy.start()
     if plan.got:
         got_load = pltpu.make_async_copy(got_hbm, got_st, got_sems.at[2])
         got_load.start()
@@ -201,11 +204,6 @@
         copy.wait()
     if first:
         build_weights(side, own_ref, oth_ref, wqkv, wqkv_t, wout_t, wout_p)
-    if not first:
-        wait_piece(0)
-        for b in range(2):
-            mask_cot(side * groups * GROUP + b * WINDOW)
-
     def base_of(i):
         return HALO + i * GROUP + side * (GROUP * groups - 3 * HALO - 2 * GROUP * i)
 
@@ -355,6 +353,12 @@
 
     wait_group(0)
     project(0, 0)
+    for copy in late:
+        copy.wait()
+    if not first:
+        wait_piece(0)
+        for b in range(2):
+            mask_cot(side * groups * GROUP + b * WINDOW)
     start = 1
     step(0, False, not first)
     if first:

time: 96.7 us -> 95.9 us (level)
  Pallas kernels: 55.5 us -> 54.3 us
    pallas_call x4, Pallas kernels: 53.6 us -> 52.4 us  [chunk_call(): pl.pallas_call(functools.partial(chunk_kernel, plan, norm), out_shape=out...]
  transfers between devices with their start and end apart: 5 -> 5, of which waited for: 3 -> 3; matrix products, arithmetic and copies ran while one was open for 0% -> 0% of each run, Pallas kernels for 40% -> 39%
where the time goes in v5:
time: 95.9 us; the launch traced here: 94.2 us
  Pallas kernels  54.3 us (57%)
  starting transfers between devices  26.2 us (27%)
  waiting for transfers between devices  8.95 us (9%)
  local copies, waits for them, and re-layouts  3.92 us (4%)
    pallas_call x4, Pallas kernels, chunk_call(): pl.pallas_call(functools.partial(chunk_kernel, plan, norm), out_shape=out...  52.4 us
    all_to_all x1, starting transfers between devices, per_device(): grads = lax.all_to_all(grads, ('head', 'gz', 'tile'), 0, 0, tiled=True)  11.7 us
    all_to_all x1, starting transfers between devices, per_device(): lax.all_to_all(share, ('gz', 'tile'), 0, 0, tiled=True).reshape(1024, 128)  8.83 us
    ppermute x1, waiting for transfers between devices, per_device(): halo = lax.ppermute(rims, ('gz', 'head', 'tile'), route)  6.44 us
    ppermute x1, starting transfers between devices, per_device(): halo = lax.ppermute(rims, ('gz', 'head', 'tile'), route)  4.4 us
    all_to_all x1, waiting for transfers between devices, per_device(): lax.all_to_all(share, ('gz', 'tile'), 0, 0, tiled=True).reshape(1024, 128)  2.01 us
    pallas_call x1, Pallas kernels, pack_call(): pl.pallas_call(pack_kernel, out_shape=(jax.ShapeDtypeStruct((1024, 128),...  1.94 us
  transfers between devices with their start and end apart: 5, of which 3 were waited for; matrix products, arithmetic and copies ran while one was open for 0% of the time, Pallas kernels for 39%

profile of v5, /device:TPU:17, one launch (start us, length us, event | category | flops | bytes accessed | tf_op | source)
XLA Modules:
  0.0 94.2 jit_solution(6125120774385288179)
XLA Ops:
  0.6 1.9 %shard_map.118 = (bf16[1024,128]{1,0:T(8,128)(2,1)}, bf16[256,512]{1,0:T(8,128)(2,1)}) custom-call(bf16[8192,256]{1,0:T(8,128)(2,1)} %refs_1_.7, bf16[8192,256]{1,0:T(8,128)(2,1)} %refs_2_.7, bf16[256,128]{1,0:T(8,128)(2,1)} %wq.1, bf16[256,128]{1,0:T(8,128)(2,1)} %wk.1, bf16[256,128]{1,0:T(8,128)(2,1)} %wv.1, bf16[128,256]{1,0:T(8,128)(2,1)} %wo.1), custom_call_target="tpu_custom_call" | custom-call | tf_op jit(solution)/shard_map/pallas_call | solution.py:524
  2.6 4.4 %collective-permute-start = (bf16[256,512]{1,0:T(8,128)(2,1)}, bf16[256,512]{1,0:T(8,128)(2,1)S(1)}, u32[]{:S(2)}, u32[]{:S(2)}) collective-permute-start(bf16[256,512]{1,0:T(8,128)(2,1)} %get-tuple-element.35), channel_id=1, source_target_pairs={{0,1},{1,2},{2,3},{3,8},{8,9},{9,10},{10,11},{11,16},{16,17},{17,1... | collective-permute-start | bytes 786440 | tf_op jit(solution)/shard_map/ppermute | solution.py:546
  7.0 0.0 collective-permute-start.1
  7.0 6.4 %collective-permute-done.refs_3_ = bf16[256,512]{1,0:T(8,128)(2,1)S(1)} collective-permute-done((bf16[256,512]{1,0:T(8,128)(2,1)}, bf16[256,512]{1,0:T(8,128)(2,1)S(1)}, u32[]{:S(2)}, u32[]{:S(2)}) %collective-permute-start) | collective-permute-done | bytes 262176 | tf_op jit(solution)/shard_map/ppermute | solution.py:546
  13.4 0.0 copy-start.1
  13.4 0.5 collective-permute-done.1.refs_5_
  13.9 0.2 copy-done.1
  14.1 0.0 copy-start.2
  14.1 0.7 copy-done.2
  14.8 15.6 %shard_map.119 = (bf16[8192,128]{1,0:T(8,128)(2,1)}, bf16[8192,128]{1,0:T(8,128)(2,1)}, bf16[1536,256]{1,0:T(8,128)(2,1)}, bf16[256,768]{1,0:T(8,128)(2,1)}, bf1...) custom-call(s32[4096]{0:T(1024)} %refs_0_.7, ...), custom_call_target="tpu_custom_call" | custom-call | flops 6144000000 | bytes 1536000 | tf_op jit(solution)/shard_map/pallas_call | solution.py:480
  30.4 1.3 %collective-permute-start.2 = (bf16[1536,256]{1,0:T(8,128)(2,1)}, bf16[1536,256]{1,0:T(8,128)(2,1)S(1)}, u32[]{:S(2)}, u32[]{:S(2)}) collective-permute-start(bf16[1536,256]{1,0:T(8,128)(2,1)} %get-tuple-element.52), channel_id=1, source_target_pairs={{0,4},{4,0},{1,5},{5,1},{2,6},{6,2},{3,7},{7,3},{8,12},{12,8},{9,1... | collective-permute-start | bytes 2359304 | tf_op jit(solution)/shard_map/ppermute | solution.py:564
  31.7 18.2 %shard_map.120 = (bf16[8192,128]{1,0:T(8,128)(2,1)}, bf16[8192,128]{1,0:T(8,128)(2,1)}, bf16[256,512]{1,0:T(8,128)(2,1)}, bf16[256,512]{1,0:T(8,128)(2,1)}, bf16...) custom-call(s32[4096]{0:T(1024)} %refs_0_.7, ...), custom_call_target="tpu_custom_call", output_to_operand_aliasing={{0}: (11, {}), {1}: (12, {})} | custom-call | flops 10240000000 | bytes 2560000 | tf_op jit(solution)/shard_map/pallas_call | solution.py:480
  49.9 11.7 %all-to-all-start = ((bf16[128,16,128]{2,1,0:T(8,128)(2,1)}), bf16[128,16,128]{2,1,0:T(8,128)(2,1)S(1)}, u32[]{:S(2)}, u32[]{:S(2)}) async-start(bf16[128,16,128]{2,1,0:T(8,128)(2,1)} %bitcast.10), calls=%async_computation | async-start | bytes 1048576 | tf_op jit(solution)/shard_map/all_to_all | solution.py:567
  61.5 0.0 collective-permute-done.2.refs_12_
  61.6 0.0 copy-start
  61.6 0.9 copy-done
  62.5 10.7 %shard_map.121 = (bf16[8192,128]{1,0:T(8,128)(2,1)}, bf16[8192,128]{1,0:T(8,128)(2,1)}, bf16[256,512]{1,0:T(8,128)(2,1)}, bf16[256,512]{1,0:T(8,128)(2,1)}, bf16[256,512]{1,0:T(8,128)(2,1)}) custom-call(s32[4096]{0:T(1024)} %refs_0_.7, bf16[8192,256]{1,0:T(8,128)(2,1)} %refs_1_.7, ...), custom_call_target="tpu_custom_call", output_to_operand_aliasing={{0}: (10, {}), {1}: (11, {})} | custom-call | flops 307200000 | bytes 1536000 | tf_op jit(solution)/shard_map/pallas_call | solution.py:480
  73.2 0.0 all-to-all-done
  73.2 0.1 reduce_sum.12
  73.3 0.7 broadcast_in_dim.2
  74.0 8.8 %all-to-all-start.1 = ((bf16[64,16,128]{2,1,0:T(8,128)(2,1)}), bf16[64,16,128]{2,1,0:T(8,128)(2,1)S(1)}, u32[]{:S(2)}, u32[]{:S(2)}) async-start(bf16[64,16,128]{2,1,0:T(8,128)(2,1)} %broadcast_in_dim.2), calls=%async_computation.1 | async-start | bytes 524288 | tf_op jit(solution)/shard_map/all_to_all | solution.py:575
  82.9 7.9 %shard_map.122 = (bf16[8192,128]{1,0:T(8,128)(2,1)}, bf16[8192,128]{1,0:T(8,128)(2,1)}) custom-call(s32[4096]{0:T(1024)} %refs_0_.7, bf16[8192,256]{1,0:T(8,128)(2,1)} %refs_1_.7, bf16[8192,256]{1,0:T(8,128)(2,1)} %refs_2_.7, bf16[256,768]{1,0:T(8,128)(2,1)} %get-tuple-element.37.refs_3_, ...), custom_call_target="tpu_custom_call", output_to_operand_aliasing={{0}: (10, {}), {1}: (11, {})} | custom-call | flops 204800000 | bytes 1024000 | tf_op jit(solution)/shard_map/pallas_call | solution.py:480
  90.7 2.0 %all-to-all-done.1 = bf16[64,16,128]{2,1,0:T(8,128)(2,1)S(1)} async-done(((bf16[64,16,128]{2,1,0:T(8,128)(2,1)}), bf16[64,16,128]{2,1,0:T(8,128)(2,1)S(1)}, u32[]{:S(2)}, u32[]{:S(2)}) %all-to-all-start.1) | async-done | bytes 262176 | tf_op jit(solution)/shard_map/all_to_all | solution.py:575
  92.8 0.7 slice_bitcast_fusion
  93.5 0.8 fusion
  (1 shorter events, 0.0 us)
Async XLA Ops:
  2.6 10.8 %collective-permute-start = (bf16[256,512]{1,0:T(8,128)(2,1)}, bf16[256,512]{1,0:T(8,128)(2,1)S(1)}, u32[]{:S(2)}, u32[]{:S(2)}) collective-permute-start(bf16[256,512]{1,0:T(8,128)(2,1)} %get-tuple-element.35), channel_id=1, source_target_pairs={{0,1},{1,2},{2,3},{3,8},{8,9},{9,10},{10,11},{11,16},{16,17},{17,1... | collective-permute-start | bytes 786440 | tf_op jit(solution)/shard_map/ppermute | solution.py:546
  7.0 6.9 %collective-permute-start.1 = (bf16[1024,128]{1,0:T(8,128)(2,1)}, bf16[1024,128]{1,0:T(8,128)(2,1)S(1)}, u32[]{:S(2)}, u32[]{:S(2)}) collective-permute-start(bf16[1024,128]{1,0:T(8,128)(2,1)} %get-tuple-element.36.refs_4_), channel_id=1, source_target_pairs={{0,4},{4,0},{1,5},{5,1},{2,6},{6,2},{3,7},{7,3},{8,12},{12,8},{9,1... | collective-permute-start | bytes 786440 | tf_op jit(solution)/shard_map/ppermute | solution.py:543
  13.4 0.7 copy-start.1
  14.1 0.7 copy-start.2
  30.4 31.1 %collective-permute-start.2 = (bf16[1536,256]{1,0:T(8,128)(2,1)}, bf16[1536,256]{1,0:T(8,128)(2,1)S(1)}, u32[]{:S(2)}, u32[]{:S(2)}) collective-permute-start(bf16[1536,256]{1,0:T(8,128)(2,1)} %get-tuple-element.52), channel_id=1, source_target_pairs={{0,4},{4,0},{1,5},{5,1},{2,6},{6,2},{3,7},{7,3},{8,12},{12,8},{9,1... | collective-permute-start | bytes 2359304 | tf_op jit(solution)/shard_map/ppermute | solution.py:564
  49.9 23.3 %all-to-all-start = ((bf16[128,16,128]{2,1,0:T(8,128)(2,1)}), bf16[128,16,128]{2,1,0:T(8,128)(2,1)S(1)}, u32[]{:S(2)}, u32[]{:S(2)}) async-start(bf16[128,16,128]{2,1,0:T(8,128)(2,1)} %bitcast.10), calls=%async_computation | async-start | bytes 1048576 | tf_op jit(solution)/shard_map/all_to_all | solution.py:567
  61.6 0.9 copy-start
  74.0 18.7 %all-to-all-start.1 = ((bf16[64,16,128]{2,1,0:T(8,128)(2,1)}), bf16[64,16,128]{2,1,0:T(8,128)(2,1)S(1)}, u32[]{:S(2)}, u32[]{:S(2)}) async-start(bf16[64,16,128]{2,1,0:T(8,128)(2,1)} %broadcast_in_dim.2), calls=%async_computation.1 | async-start | bytes 524288 | tf_op jit(solution)/shard_map/all_to_all | solution.py:575
